TPU v7x, 32 devices: a whole 2x2x4 slice. The times are simulated.
32 devices in a mesh: sec: 16 (over z, y, x), tile: 2 (over core).
Axes of the slice: x: 2, y: 2, z: 4, core: 2. Of those that a mesh axis runs over, the one named last changes fastest.
Arguments:
- sections: bfloat16 [16, 256, 4096], P('sec', None, 'tile'), may hold values from -120 to 120, as said below
- calibration_knots: int32 [17], replicated, may hold values from 200 to 8200, as said below
- target_offset: int32 [4, 64], P(None, 'tile'), may hold values from 0 to 63
- target_step: int32 [4, 64], P(None, 'tile'), may hold values from 32 to 63
Outputs:
- resampled: bfloat16 [16, 256, 4096], P(None, 'sec', 'tile')
Inputs may be any that keep to these rules, and one draw needn't show every extreme that they name: sections are intensities correlated from section to section. calibration_knots fall strictly from the first knot, 8200, to the last, 200.
All inputs are finite; a program needn't handle non-finite values.
Results may differ from a plain program's by a relative error of at most 0.0044.
Values may be sent and summed in bfloat16 or wider, within the bound.
No kernel may reach another device: no remote copies, remote signals or barrier semaphores. Data moves between devices by JAX's collectives and lax.ppermute only.
A program may use at most 256 MiB of HBM per device.

v0:
```python
import jax
import jax.numpy as jnp
from jax import lax
from jax.sharding import PartitionSpec as P

TILE = 64
AHEAD = 4


epsilon = 1e-06


def from_behind(value, axis, steps):
    count = lax.axis_size(axis)
    first, last = (max(0, -steps), min(count, count - steps))
    return lax.ppermute(value, axis, [(source, source + steps) for source in range(first, last)])


def shrink(pixels):
    leading = pixels.shape[:-2]
    row_total = pixels.shape[-2]
    col_total = pixels.shape[-1]
    blocks = pixels.astype(jnp.float32).reshape(leading + (row_total // 2, 2, col_total // 2, 2))
    return jnp.mean(blocks, axis=(-3, -1)).astype(jnp.bfloat16)


def moments(current, following, row_group, half_tile):
    leading = current.shape[:-2]
    tiled_shape = leading + (
        current.shape[-2] // row_group,
        row_group,
        current.shape[-1] // half_tile,
        half_tile,
    )
    first_tile = current.astype(jnp.float32).reshape(tiled_shape)
    second_tile = following.astype(jnp.float32).reshape(tiled_shape)

    def tile_total(values):
        return jnp.sum(values, axis=(-3, -1))

    return (
        tile_total(first_tile),
        tile_total(second_tile),
        tile_total(first_tile * first_tile),
        tile_total(second_tile * second_tile),
        tile_total(first_tile * second_tile),
    )


def correlate(moment_sums, samples):
    sum_first, sum_second, sum_ff, sum_ss, sum_fs = moment_sums
    mean_first = sum_first / samples
    mean_second = sum_second / samples
    covariance = sum_fs / samples - mean_first * mean_second
    var_first = sum_ff / samples - mean_first * mean_first
    var_second = sum_ss / samples - mean_second * mean_second
    return covariance / jnp.sqrt(var_first * var_second + epsilon)


def calibrate(correlation, knot_values):
    knot_total = knot_values.shape[0]
    knot_grid = -1.0 + jnp.arange(knot_total, dtype=jnp.float32) * (2.0 / (knot_total - 1))
    hat_weights = jnp.maximum(
        0.0, 1.0 - jnp.abs(correlation[..., None] - knot_grid) * ((knot_total - 1) / 2.0)
    )
    return jnp.sum(hat_weights * (knot_values.astype(jnp.float32) / 1000.0), axis=-1)


def exclusive_last(values):
    running = jnp.cumsum(values, axis=-1)
    return jnp.concatenate(
        [jnp.zeros(values.shape[:-1] + (1,), jnp.float32), running[..., :-1]], axis=-1
    )


def resample_weights(depths, offsets, strides, outputs):
    section_total = depths.shape[-1]
    grid_index = jnp.arange(outputs, dtype=jnp.int32)
    fraction = (offsets[..., None] + grid_index * strides[..., None]).astype(jnp.float32) / (
        64.0 * outputs
    )
    target = depths[..., -1:] * fraction
    bracket = jnp.sum((depths[..., None, 1:] <= target[..., None]).astype(jnp.int32), axis=-1)
    bracket = jnp.minimum(bracket, section_total - 2)
    section_places = jnp.arange(section_total, dtype=jnp.int32)
    lower_depth = jnp.sum(
        jnp.where(section_places == bracket[..., None], depths[..., None, :], 0.0), axis=-1
    )
    upper_depth = jnp.sum(
        jnp.where(section_places == bracket[..., None] + 1, depths[..., None, :], 0.0), axis=-1
    )
    lifted = bracket.astype(jnp.float32) + (target - lower_depth) / (upper_depth - lower_depth)
    spread = jnp.abs(lifted[..., None] - section_places.astype(jnp.float32))
    return jnp.maximum(0.0, 1.0 - spread).astype(jnp.bfloat16)


def per_device(sections, calibration_knots, target_offset, target_step):
    section_total = lax.axis_size("sec")
    position = lax.axis_index("sec")
    half_tile = TILE // 2
    samples = float(half_tile * half_tile)
    row_total = sections.shape[1]
    rows_local = row_total // section_total
    tile_rows = row_total // TILE
    tiles_wide = sections.shape[2] // TILE
    tile_row = position * rows_local // TILE
    pencils = lax.all_to_all(sections, "sec", split_axis=1, concat_axis=0, tiled=True)
    reduced = shrink(sections[0])
    numerator = jnp.zeros((tile_rows, tiles_wide), jnp.float32)
    denominator = jnp.zeros((), jnp.float32)
    for spacing in range(1, AHEAD + 1):
        forward = from_behind(reduced, "sec", -spacing)
        correlation = correlate(moments(reduced, forward, half_tile, half_tile), samples)
        usable = (position + spacing < section_total).astype(jnp.float32)
        numerator = numerator + usable * (spacing * calibrate(correlation, calibration_knots))
        denominator = denominator + usable * float(spacing * spacing)
    thickness = numerator / jnp.maximum(denominator, 1.0)
    spread_rows = jnp.repeat(thickness, TILE, axis=0)[None]
    carried_maps = lax.all_to_all(spread_rows, "sec", split_axis=1, concat_axis=0, tiled=True)
    column_maps = jnp.transpose(carried_maps[:, 0, :])
    depths = exclusive_last(column_maps)
    offsets_row = lax.dynamic_index_in_dim(target_offset, tile_row, 0, keepdims=False)
    strides_row = lax.dynamic_index_in_dim(target_step, tile_row, 0, keepdims=False)
    weights = resample_weights(depths, offsets_row, strides_row, section_total)
    pencil_tiles = pencils.reshape(section_total, rows_local, tiles_wide, TILE)
    resampled = jnp.einsum(
        "tjs,srtc->jrtc", weights, pencil_tiles, preferred_element_type=jnp.float32
    )
    return resampled.reshape(section_total, rows_local, sections.shape[2]).astype(jnp.bfloat16)


def solution(mesh):
    return jax.shard_map(
        per_device,
        mesh=mesh,
        in_specs=(P("sec", None, "tile"), P(), P(None, "tile"), P(None, "tile")),
        out_specs=P(None, "sec", "tile"),
        check_vma=False,
    )
```

profile of v0, /device:TPU:0, one launch (start us, length us, event | category | flops | bytes accessed | tf_op | source)
XLA Modules:
  0.0 279.6 jit_solution(7261011828329150954)
XLA Ops:
  0.0 137.6 %reshape.290 = f32[128,2,1024,2]{3,2,1,0:T(8,128)} reshape(bf16[1,256,2048]{2,1,0:T(8,128)(2,1)} %param.4) | data formatting | bytes 3145728 | tf_op jit(solution)/shard_map/convert_element_type | solution.py:23
  137.6 40.9 %reduce_sum.191 = f32[128,1024]{1,0:T(8,128)S(1)} reduce(f32[128,2,1024,2]{3,2,1,0:T(8,128)} %reshape.290, f32[]{:T(128)} %constant.81.clone.1), dimensions={1,3}, to_apply=%region_0.1 | reduce | flops 393216 | bytes 2621444 | tf_op jit(solution)/shard_map/reduce_sum | solution.py:24
  178.5 0.0 copy-start.1
  178.5 1.3 collective-permute-start
  179.8 1.3 collective-permute-start.1
  181.1 1.3 collective-permute-start.2
  182.4 1.3 collective-permute-start.3
  183.7 0.7 reshape.291
  184.5 5.2 %collective-permute-done = bf16[128,1024]{1,0:T(8,128)(2,1)S(1)} collective-permute-done((bf16[128,1024]{1,0:T(8,128)(2,1)S(1)}, bf16[128,1024]{1,0:T(8,128)(2,1)S(1)}, u32[]{:S(2)}, u32[]{:S(2)}) %collective-permute-start) | collective-permute-done | bytes 262176 | tf_op jit(solution)/shard_map/ppermute | solution.py:16
  189.7 2.0 reshape.293
  191.7 6.7 %collective-permute-done.1 = bf16[128,1024]{1,0:T(8,128)(2,1)S(1)} collective-permute-done((bf16[128,1024]{1,0:T(8,128)(2,1)S(1)}, bf16[128,1024]{1,0:T(8,128)(2,1)S(1)}, u32[]{:S(2)}, u32[]{:S(2)}) %collective-permute-start.1) | collective-permute-done | bytes 262176 | tf_op jit(solution)/shard_map/ppermute | solution.py:16
  198.4 2.0 reshape.295
  200.5 2.0 reshape.297
  202.5 7.3 %collective-permute-done.3 = bf16[128,1024]{1,0:T(8,128)(2,1)S(1)} collective-permute-done((bf16[128,1024]{1,0:T(8,128)(2,1)S(1)}, bf16[128,1024]{1,0:T(8,128)(2,1)S(1)}, u32[]{:S(2)}, u32[]{:S(2)}) %collective-permute-start.3) | collective-permute-done | bytes 262176 | tf_op jit(solution)/shard_map/ppermute | solution.py:16
  209.8 2.0 reshape.299
  211.8 5.0 %multiply_reduce_fusion.8 = (f32[4,32]{1,0:T(4,128)S(1)}, f32[4,32]{1,0:T(4,128)S(1)}, f32[4,32]{1,0:T(4,128)S(1)}, f32[4,32]{1,0:T(4,128)S(1)}, f32[4,32]{1,0:T...) fusion(f32[4,32,32,32]{3,2,1,0:T(8,128)S(1)} %reshape.291, ...), kind=kLoop, calls=%fused_computation.11 | loop fusion | flops 3012864 | bytes 2628608 | tf_op jit(solution)/shard_map/reduce_sum | solution.py:39
  216.8 0.2 multiply_reduce_fusion.12
  217.0 0.5 broadcast.288
  217.6 1.0 reduce.5
  218.5 0.7 reshape.305
  219.2 4.0 %all-to-all-start = ((f32[16,1,512]{2,1,0:T(1,128)}), f32[16,1,512]{2,1,0:T(1,128)S(1)}, u32[]{:S(2)}, u32[]{:S(2)}) async-start(f32[16,1,512]{2,1,0:T(1,128)} %reshape.305), calls=%async_computation | async-start | bytes 65536 | tf_op jit(solution)/shard_map/all_to_all | solution.py:119
  223.2 1.6 copy.37
  224.9 0.5 broadcast.287
  225.4 6.8 %reduce.4 = bf16[256,2048]{1,0:T(8,128)(2,1)S(1)} reduce(bf16[256,1,2048]{2,1,0:T(2,128)(2,1)S(1)} %bitcast.26, bf16[]{:T(256)} %broadcast.287), dimensions={1}, to_apply=%bitcast.24.reduce_sub_computation | reduce | bytes 2097154
  232.2 1.6 reshape.303
  233.8 0.0 all-to-all-done
  233.8 6.9 %all-to-all-start.1 = ((bf16[16,2,16384]{2,1,0:T(2,128)(2,1)}), bf16[16,2,16384]{2,1,0:T(2,128)(2,1)S(1)}, u32[]{:S(2)}, u32[]{:S(2)}) async-start(bf16[16,2,16384]{2,1,0:T(2,128)(2,1)} %reshape.303), calls=%async_computation.1 | async-start | bytes 2097152 | tf_op jit(solution)/shard_map/all_to_all | solution.py:107
  240.7 0.7 dynamic-slice_bitcast_fusion
  241.4 0.7 reduce.6
  242.1 0.2 reshape.306
  242.4 0.1 copy.20
  242.5 0.2 reduce_window_sum.11
  242.6 0.1 copy.21
  242.7 0.1 concatenate.3
  242.8 0.2 fusion.10
  243.0 0.1 copy.22
  243.1 0.1 copy.24
  243.2 0.4 select_reduce_fusion.1
  243.5 0.1 copy.23
  243.6 0.1 copy.25
  243.7 0.1 copy.27
  243.8 19.9 %all-to-all-done.1 = bf16[16,2,16384]{2,1,0:T(2,128)(2,1)S(1)} async-done(((bf16[16,2,16384]{2,1,0:T(2,128)(2,1)}), bf16[16,2,16384]{2,1,0:T(2,128)(2,1)S(1)}, u32[]{:S(2)}, u32[]{:S(2)}) %all-to-all-start.1) | async-done | bytes 1048608 | tf_op jit(solution)/shard_map/all_to_all | solution.py:107
  263.7 1.0 reshape.304
  264.7 6.1 %bitcast_reduce_fusion = bf16[256,2048]{1,0:T(8,128)(2,1)S(1)} fusion(bf16[256,1,2048]{2,1,0:T(2,128)(2,1)S(1)} %reshape.304), kind=kLoop, calls=%fused_computation.47 | loop fusion | bytes 2097152 | tf_op jit(solution)/shard_map/all_to_all | solution.py:107
  270.8 2.4 reshape.289
  273.3 2.6 convert_bitcast_fusion
  275.8 1.4 copy.30
  277.2 2.4 convert_element_type.95
  (15 shorter events, 0.2 us)
Async XLA Ops:
  178.5 6.0 %copy-start.1 = (s32[17]{0:T(128)S(1)}, s32[17]{0:T(128)}, u32[]{:S(2)}) copy-start(s32[17]{0:T(128)} %param.5) | copy-start | bytes 208
  178.5 11.1 %collective-permute-start = (bf16[128,1024]{1,0:T(8,128)(2,1)S(1)}, bf16[128,1024]{1,0:T(8,128)(2,1)S(1)}, u32[]{:S(2)}, u32[]{:S(2)}) collective-permute-start(bf16[128,1024]{1,0:T(8,128)(2,1)S(1)} %multiply_convert_fusion), channel_id=1, source_target_pairs={{2,0},{4,2},{6,4},{8,6},{10,8},{12,10},{14,12},{16,14},{18,16},{20... | collective-permute-start | bytes 786440 | tf_op jit(solution)/shard_map/ppermute | solution.py:16
  179.8 18.6 %collective-permute-start.1 = (bf16[128,1024]{1,0:T(8,128)(2,1)S(1)}, bf16[128,1024]{1,0:T(8,128)(2,1)S(1)}, u32[]{:S(2)}, u32[]{:S(2)}) collective-permute-start(bf16[128,1024]{1,0:T(8,128)(2,1)S(1)} %multiply_convert_fusion), channel_id=1, source_target_pairs={{4,0},{6,2},{8,4},{10,6},{12,8},{14,10},{16,12},{18,14},{20,16},{2... | collective-permute-start | bytes 786440 | tf_op jit(solution)/shard_map/ppermute | solution.py:16
  181.1 19.3 %collective-permute-start.2 = (bf16[128,1024]{1,0:T(8,128)(2,1)S(1)}, bf16[128,1024]{1,0:T(8,128)(2,1)S(1)}, u32[]{:S(2)}, u32[]{:S(2)}) collective-permute-start(bf16[128,1024]{1,0:T(8,128)(2,1)S(1)} %multiply_convert_fusion), channel_id=1, source_target_pairs={{6,0},{8,2},{10,4},{12,6},{14,8},{16,10},{18,12},{20,14},{22,16},{... | collective-permute-start | bytes 786440 | tf_op jit(solution)/shard_map/ppermute | solution.py:16
  182.4 27.3 %collective-permute-start.3 = (bf16[128,1024]{1,0:T(8,128)(2,1)S(1)}, bf16[128,1024]{1,0:T(8,128)(2,1)S(1)}, u32[]{:S(2)}, u32[]{:S(2)}) collective-permute-start(bf16[128,1024]{1,0:T(8,128)(2,1)S(1)} %multiply_convert_fusion), channel_id=1, source_target_pairs={{8,0},{10,2},{12,4},{14,6},{16,8},{18,10},{20,12},{22,14},{24,16},... | collective-permute-start | bytes 786440 | tf_op jit(solution)/shard_map/ppermute | solution.py:16
  211.8 11.5 %copy-start = (bf16[1,256,2048]{2,1,0:T(8,128)(2,1)S(1)}, bf16[1,256,2048]{2,1,0:T(8,128)(2,1)}, u32[]{:S(2)}) copy-start(bf16[1,256,2048]{2,1,0:T(8,128)(2,1)} %param.4) | copy-start | bytes 3145732
  219.2 14.5 %all-to-all-start = ((f32[16,1,512]{2,1,0:T(1,128)}), f32[16,1,512]{2,1,0:T(1,128)S(1)}, u32[]{:S(2)}, u32[]{:S(2)}) async-start(f32[16,1,512]{2,1,0:T(1,128)} %reshape.305), calls=%async_computation | async-start | bytes 65536 | tf_op jit(solution)/shard_map/all_to_all | solution.py:119
  233.8 29.9 %all-to-all-start.1 = ((bf16[16,2,16384]{2,1,0:T(2,128)(2,1)}), bf16[16,2,16384]{2,1,0:T(2,128)(2,1)S(1)}, u32[]{:S(2)}, u32[]{:S(2)}) async-start(bf16[16,2,16384]{2,1,0:T(2,128)(2,1)} %reshape.303), calls=%async_computation.1 | async-start | bytes 2097152 | tf_op jit(solution)/shard_map/all_to_all | solution.py:107
where the time goes:
time: 280 us
  local copies, waits for them, and re-layouts  166 us (59%)
  other arithmetic  55.4 us (20%)
  waiting for transfers between devices  39.1 us (14%)
  starting transfers between devices  16.1 us (6%)
    convert_element_type x1, local copies, waits for them, and re-layouts, shrink(): pixels.astype(jnp.float32)  138 us
    reduce_sum x1, other arithmetic, shrink(): return jnp.mean(blocks, axis=(-3, -1)).astype(jnp.bfloat16)  40.9 us
    all_to_all x1, waiting for transfers between devices, per_device(): lax.all_to_all(sections, 'sec', split_axis=1, concat_axis=0, tiled=True)  19.9 us
    ppermute x4, waiting for transfers between devices, from_behind(): lax.ppermute(value, axis, [(source, source + steps) for source in range(f...  19.2 us
    reshape x4, local copies, waits for them, and re-layouts, moments(): second_tile = following.astype(jnp.float32).reshape(tiled_shape)  8.1 us
    unnamed x2, other arithmetic  7.75 us
    all_to_all x1, starting transfers between devices, per_device(): lax.all_to_all(sections, 'sec', split_axis=1, concat_axis=0, tiled=True)  6.91 us
    unnamed x11, local copies, waits for them, and re-layouts  6.24 us
  transfers between devices with their start and end apart: 6, of which 4 were waited for; matrix products, arithmetic and copies ran while one was open for 7% of the time, Pallas kernels for 0%

commit v1 on v0

--- a/solution.py
+++ b/solution.py
@@ -1,13 +1,16 @@
+import functools
+
 import jax
 import jax.numpy as jnp
 from jax import lax
+from jax.experimental import pallas as pl
+from jax.experimental.pallas import tpu as pltpu
 from jax.sharding import PartitionSpec as P
 
 TILE = 64
 AHEAD = 4
-
-
-epsilon = 1e-06
+LANES = 128
+EPSILON = 1e-06
 
 
 def from_behind(value, axis, steps):
@@ -54,7 +57,7 @@
     covariance = sum_fs / samples - mean_first * mean_second
     var_first = sum_ff / samples - mean_first * mean_first
     var_second = sum_ss / samples - mean_second * mean_second
-    return covariance / jnp.sqrt(var_first * var_second + epsilon)
+    return covariance / jnp.sqrt(var_first * var_second + EPSILON)
 
 
 def calibrate(correlation, knot_values):
@@ -94,7 +97,7 @@
     return jnp.maximum(0.0, 1.0 - spread).astype(jnp.bfloat16)
 
 
-def per_device(sections, calibration_knots, target_offset, target_step):
+def plain_per_device(sections, calibration_knots, target_offset, target_step):
     section_total = lax.axis_size("sec")
     position = lax.axis_index("sec")
     half_tile = TILE // 2
@@ -129,6 +132,190 @@
     return resampled.reshape(section_total, rows_local, sections.shape[2]).astype(jnp.bfloat16)
 
 
+def one_hot(shape, row_of, col_of):
+    rows = lax.broadcasted_iota(jnp.int32, shape, 0)
+    cols = lax.broadcasted_iota(jnp.int32, shape, 1)
+    return (row_of(rows) == col_of(cols)).astype(jnp.float32).astype(jnp.bfloat16)
+
+
+def shift_up(values, steps):
+    if steps == 0:
+        return values
+    return jnp.concatenate([values[steps:], jnp.zeros_like(values[:steps])], axis=0)
+
+
+def split_dot(values, ones):
+    high = values.astype(jnp.bfloat16)
+    rest = values - high.astype(jnp.float32)
+    middle = rest.astype(jnp.bfloat16)
+    low = (rest - middle.astype(jnp.float32)).astype(jnp.bfloat16)
+    dot = functools.partial(jnp.dot, preferred_element_type=jnp.float32)
+    return dot(high, ones) + (dot(middle, ones) + dot(low, ones))
+
+
+def sums_kernel(x_ref, sums_ref, pairs_ref, totals_ref):
+    sections, rows, cols = x_ref.shape
+    half = cols // 2
+    tiles = cols // TILE
+    pairing = one_hot((2 * LANES, LANES), lambda r: r // 2, lambda c: c)
+    for g in range(half // LANES):
+        wide = x_ref[:, :, 2 * LANES * g : 2 * LANES * (g + 1)]
+        pairs_ref[g] = jnp.dot(
+            wide.reshape(sections * rows, 2 * LANES),
+            pairing,
+            preferred_element_type=jnp.float32,
+        )
+    for g in range(half // LANES):
+        lanes = pl.ds(LANES * g, LANES)
+        totals = [jnp.zeros((sections, LANES), jnp.float32)] * (AHEAD + 2)
+        for r in range(rows // 2):
+            upper = pairs_ref[g, pl.ds(2 * r, sections, stride=rows), :]
+            lower = pairs_ref[g, pl.ds(2 * r + 1, sections, stride=rows), :]
+            reduced = ((upper + lower) * 0.25).astype(jnp.bfloat16).astype(jnp.float32)
+            totals[0] = totals[0] + reduced
+            for k in range(AHEAD + 1):
+                totals[k + 1] = totals[k + 1] + reduced * shift_up(reduced, k)
+        for q in range(AHEAD + 2):
+            totals_ref[sections * q : sections * (q + 1), lanes] = totals[q]
+    of_tile = one_hot((half, tiles), lambda r: r // (TILE // 2), lambda c: c)
+    sums = split_dot(totals_ref[...], of_tile)
+    wide = LANES // tiles
+    height = sums.shape[0] // wide
+    for q in range(wide):
+        sums_ref[:, tiles * q : tiles * (q + 1)] = sums[height * q : height * (q + 1)]
+
+
+def resample_kernel(
+    tile_row_ref, knots_ref, offset_ref, step_ref, *refs
+):
+    *sums_refs, x_ref, out_ref, weights_ref, spread_ref = refs
+    sections, rows, cols = x_ref.shape
+    outputs = out_ref.shape[0]
+    tiles = cols // TILE
+    samples = float((TILE // 2) ** 2)
+    packed = sums_refs[0][...]
+    for ref in sums_refs[1:]:
+        packed = packed + ref[...]
+    parts = LANES // tiles
+    sums = jnp.concatenate(
+        [packed[:, tiles * q : tiles * (q + 1)] for q in range(parts)], axis=0
+    )
+    quantity = [sums[sections * q : sections * (q + 1)] for q in range(AHEAD + 2)]
+    mean = quantity[0] / samples
+    variance = quantity[1] / samples - mean * mean
+    place = lax.broadcasted_iota(jnp.int32, (sections, tiles), 0)
+    numerator = jnp.zeros((sections, tiles), jnp.float32)
+    denominator = jnp.zeros((sections, tiles), jnp.float32)
+    knots = knots_ref.shape[0]
+    for k in range(1, AHEAD + 1):
+        covariance = quantity[k + 1] / samples - mean * shift_up(mean, k)
+        correlation = covariance / jnp.sqrt(variance * shift_up(variance, k) + EPSILON)
+        distance = jnp.zeros((sections, tiles), jnp.float32)
+        for j in range(knots):
+            grid = -1.0 + j * (2.0 / (knots - 1))
+            hat = jnp.maximum(0.0, 1.0 - jnp.abs(correlation - grid) * ((knots - 1) / 2.0))
+            distance = distance + hat * (knots_ref[j].astype(jnp.float32) / 1000.0)
+        usable = (place + k < sections).astype(jnp.float32)
+        numerator = numerator + usable * (k * distance)
+        denominator = denominator + usable * float(k * k)
+    thickness = numerator / jnp.maximum(denominator, 1.0)
+    depths = [jnp.zeros((1, tiles), jnp.float32)]
+    for s in range(sections - 1):
+        depths.append(depths[-1] + thickness[s : s + 1])
+    row = tile_row_ref[0]
+    offset = offset_ref[pl.ds(row, 1), :]
+    step = step_ref[pl.ds(row, 1), :]
+    index = lax.broadcasted_iota(jnp.int32, (outputs, tiles), 0)
+    fraction = (offset + index * step).astype(jnp.float32) / (64.0 * outputs)
+    target = depths[-1] * fraction
+    bracket = jnp.zeros((outputs, tiles), jnp.int32)
+    for s in range(1, sections):
+        bracket = bracket + (depths[s] <= target).astype(jnp.int32)
+    bracket = jnp.minimum(bracket, sections - 2)
+    lower = jnp.zeros((outputs, tiles), jnp.float32)
+    upper = jnp.zeros((outputs, tiles), jnp.float32)
+    for s in range(sections - 1):
+        here = bracket == s
+        lower = jnp.where(here, depths[s], lower)
+        upper = jnp.where(here, depths[s + 1], upper)
+    lifted = bracket.astype(jnp.float32) + (target - lower) / (upper - lower)
+    for s in range(sections):
+        weights_ref[outputs * s : outputs * (s + 1), :] = jnp.maximum(
+            0.0, 1.0 - jnp.abs(lifted - float(s))
+        ).astype(jnp.bfloat16)
+    to_pixels = one_hot((tiles, cols), lambda r: r, lambda c: c // TILE)
+    spread_ref[...] = jnp.dot(
+        weights_ref[...], to_pixels, preferred_element_type=jnp.float32
+    )
+
+    @pl.loop(0, cols // LANES)
+    def _(g):
+        lanes = pl.ds(pl.multiple_of(g * LANES, LANES), LANES)
+        pixels = [x_ref[s, :, lanes].astype(jnp.float32) for s in range(sections)]
+        for j in range(outputs):
+            total = jnp.zeros((rows, LANES), jnp.float32)
+            for s in range(sections):
+                total = total + spread_ref[pl.ds(outputs * s + j, 1), lanes] * pixels[s]
+            out_ref[j, :, lanes] = total.astype(jnp.bfloat16)
+
+
+def per_device(sections, calibration_knots, target_offset, target_step):
+    section_total = lax.axis_size("sec")
+    position = lax.axis_index("sec")
+    row_total, cols = sections.shape[1:]
+    rows_local = row_total // section_total
+    sharers = TILE // rows_local
+    tiles = cols // TILE
+    if rows_local % 16 or section_total % 8 or LANES % tiles or cols % (2 * LANES):
+        return plain_per_device(
+            sections, calibration_knots, target_offset, target_step
+        )
+    blocks = sections.reshape(section_total, rows_local, cols)
+    pencils = lax.all_to_all(blocks, "sec", split_axis=0, concat_axis=0, tiled=True)
+    height = (AHEAD + 2) * section_total * tiles // LANES
+    vmem = pl.BlockSpec(memory_space=pltpu.VMEM)
+    smem = pl.BlockSpec(memory_space=pltpu.SMEM)
+    pixels = section_total * rows_local * cols
+    partial_sums = pl.pallas_call(
+        sums_kernel,
+        out_shape=jax.ShapeDtypeStruct((height, LANES), jnp.float32),
+        in_specs=[vmem],
+        out_specs=vmem,
+        scratch_shapes=[
+            pltpu.VMEM(
+                (cols // 2 // LANES, section_total * rows_local, LANES), jnp.float32
+            ),
+            pltpu.VMEM(((AHEAD + 2) * section_total, cols // 2), jnp.float32),
+        ],
+        compiler_params=pltpu.CompilerParams(vmem_limit_bytes=32 * 2**20),
+        cost_estimate=pl.CostEstimate(
+            flops=pixels * 8, bytes_accessed=pixels * 2, transcendentals=0
+        ),
+    )(pencils)
+    all_sums = [partial_sums]
+    for other in range(1, sharers):
+        all_sums.append(
+            lax.ppermute(
+                partial_sums, "sec", [(i, i ^ other) for i in range(section_total)]
+            )
+        )
+    tile_row = (position * rows_local // TILE).astype(jnp.int32).reshape(1)
+    return pl.pallas_call(
+        resample_kernel,
+        out_shape=jax.ShapeDtypeStruct(pencils.shape, jnp.bfloat16),
+        in_specs=[smem, smem, vmem, vmem] + [vmem] * sharers + [vmem],
+        out_specs=vmem,
+        scratch_shapes=[
+            pltpu.VMEM((section_total * section_total, tiles), jnp.bfloat16),
+            pltpu.VMEM((section_total * section_total, cols), jnp.float32),
+        ],
+        compiler_params=pltpu.CompilerParams(vmem_limit_bytes=32 * 2**20),
+        cost_estimate=pl.CostEstimate(
+            flops=pixels * 2 * section_total, bytes_accessed=pixels * 4, transcendentals=0
+        ),
+    )(tile_row, calibration_knots, target_offset, target_step, *all_sums, pencils)
+
+
 def solution(mesh):
     return jax.shard_map(
         per_device,

time: 280 us -> 46.9 us (0.17)
  local copies, waits for them, and re-layouts: 166 us -> 0.01 us
  other arithmetic: 55.4 us -> 0 us
  waiting for transfers between devices: 39.1 us -> 2.22 us
  blocking collectives: 0 us -> 34.7 us
  starting transfers between devices: 16.1 us -> 3.55 us
  Pallas kernels: 0 us -> 6.22 us
    convert_element_type x4 -> x0, local copies, waits for them, and re-layouts: 142 us -> none  [the longest x1 138 us: shrink(): pixels.astype(jnp.float32)]
    reduce_sum x5 -> x0, other arithmetic: 46.4 us -> none  [the longest x1 40.9 us: shrink(): return jnp.mean(blocks, axis=(-3, -1)).astype(jnp.bfloat16)]
    all_to_all x0 -> x1, blocking collectives: none -> 34.7 us  [per_device(): lax.all_to_all(blocks, 'sec', split_axis=0, concat_axis=0, tiled=True)]
    all_to_all x2 -> x0, waiting for transfers between devices: 19.9 us -> none  [the longest x1 19.9 us: per_device(): lax.all_to_all(sections, 'sec', split_axis=1, concat_axis=0, tiled=True)]
    ppermute x4 -> x3, waiting for transfers between devices: 19.2 us -> 2.22 us  [per_device(): lax.ppermute(partial_sums, 'sec', [(i, i ^ other) for i in range(section_...]
    all_to_all x2 -> x0, starting transfers between devices: 10.9 us -> none  [the longest x1 6.91 us: per_device(): lax.all_to_all(sections, 'sec', split_axis=1, concat_axis=0, tiled=True)]
    reshape x5 -> x0, local copies, waits for them, and re-layouts: 10.6 us -> none  [the longest x4 8.1 us: moments(): second_tile = following.astype(jnp.float32).reshape(tiled_shape)]
    unnamed x2 -> x0, other arithmetic: 7.75 us -> none
  transfers between devices with their start and end apart: 6 -> 3, of which waited for: 4 -> 3; matrix products, arithmetic and copies ran while one was open for 7% -> 0% of each run, Pallas kernels for 0% -> 0%
where the time goes in v1:
time: 46.9 us; the launch traced here: 46.7 us
  blocking collectives  34.7 us (74%)
  Pallas kernels  6.22 us (13%)
  starting transfers between devices  3.55 us (8%)
  waiting for transfers between devices  2.22 us (5%)
    all_to_all x1, blocking collectives, per_device(): lax.all_to_all(blocks, 'sec', split_axis=0, concat_axis=0, tiled=True)  34.7 us
    pallas_call x1, Pallas kernels, per_device(): pl.pallas_call(resample_kernel, out_shape=jax.ShapeDtypeStruct(pencils.sh...  4.94 us
    ppermute x3, starting transfers between devices, per_device(): lax.ppermute(partial_sums, 'sec', [(i, i ^ other) for i in range(section_...  3.55 us
    ppermute x3, waiting for transfers between devices, per_device(): lax.ppermute(partial_sums, 'sec', [(i, i ^ other) for i in range(section_...  2.22 us
    pallas_call x1, Pallas kernels, per_device(): pl.pallas_call(sums_kernel, out_shape=jax.ShapeDtypeStruct((height, LANES...  1.28 us
  transfers between devices with their start and end apart: 3, of which 3 were waited for; matrix products, arithmetic and copies ran while one was open for 0% of the time, Pallas kernels for 0%

profile of v1, /device:TPU:0, one launch (start us, length us, event | category | flops | bytes accessed | tf_op | source)
XLA Modules:
  0.0 46.7 jit_solution(3013156113386853591)
XLA Ops:
  0.0 34.7 %all_to_all.5.x_ref.refs_4_ = bf16[16,16,2048]{2,1,0:T(8,128)(2,1)S(1)} all-to-all(bf16[16,16,2048]{2,1,0:T(8,128)(2,1)} %bitcast.2), channel_id=1, replica_groups=mesh['sec'=16,'tile'=2] {'sec'}, dimensions={0} | all-to-all | bytes 2097152 | tf_op jit(solution)/shard_map/all_to_all | solution.py:274
  34.7 1.3 %shard_map.46.refs_0_ = f32[24,128]{1,0:T(8,128)S(1)} custom-call(bf16[16,16,2048]{2,1,0:T(8,128)(2,1)S(1)} %all_to_all.5.x_ref.refs_4_), custom_call_target="tpu_custom_call" | custom-call | flops 4194304 | bytes 1048576 | tf_op jit(solution)/shard_map/pallas_call | solution.py:279
  36.0 1.0 %collective-permute-start.2 = (f32[24,128]{1,0:T(8,128)S(1)}, f32[24,128]{1,0:T(8,128)S(1)}, u32[]{:S(2)}, u32[]{:S(2)}) collective-permute-start(f32[24,128]{1,0:T(8,128)S(1)} %shard_map.46.refs_0_), channel_id=1, source_target_pairs={{0,6},{2,4},{4,2},{6,0},{8,14},{10,12},{12,10},{14,8},{16,22},{18,... | collective-permute-start | bytes 36872 | tf_op jit(solution)/shard_map/ppermute | solution.py:298
  36.9 1.1 %collective-permute-start.1 = (f32[24,128]{1,0:T(8,128)S(1)}, f32[24,128]{1,0:T(8,128)S(1)}, u32[]{:S(2)}, u32[]{:S(2)}) collective-permute-start(f32[24,128]{1,0:T(8,128)S(1)} %shard_map.46.refs_0_), channel_id=1, source_target_pairs={{0,4},{2,6},{4,0},{6,2},{8,12},{10,14},{12,8},{14,10},{16,20},{18,... | collective-permute-start | bytes 36872 | tf_op jit(solution)/shard_map/ppermute | solution.py:298
  38.1 1.5 %collective-permute-start = (f32[24,128]{1,0:T(8,128)S(1)}, f32[24,128]{1,0:T(8,128)S(1)}, u32[]{:S(2)}, u32[]{:S(2)}) collective-permute-start(f32[24,128]{1,0:T(8,128)S(1)} %shard_map.46.refs_0_), channel_id=1, source_target_pairs={{0,2},{2,0},{4,6},{6,4},{8,10},{10,8},{12,14},{14,12},{16,18},{18,... | collective-permute-start | bytes 36872 | tf_op jit(solution)/shard_map/ppermute | solution.py:298
  39.5 0.0 copy-start.1
  39.5 0.0 copy-start
  39.5 0.0 copy-start.2
  39.5 1.1 %collective-permute-done.2.refs_3_ = f32[24,128]{1,0:T(8,128)S(1)} collective-permute-done((f32[24,128]{1,0:T(8,128)S(1)}, f32[24,128]{1,0:T(8,128)S(1)}, u32[]{:S(2)}, u32[]{:S(2)}) %collective-permute-start.2) | collective-permute-done | bytes 12320 | tf_op jit(solution)/shard_map/ppermute | solution.py:298
  40.6 0.1 collective-permute-done.1.refs_2_
  40.8 1.0 %collective-permute-done.refs_1_ = f32[24,128]{1,0:T(8,128)S(1)} collective-permute-done((f32[24,128]{1,0:T(8,128)S(1)}, f32[24,128]{1,0:T(8,128)S(1)}, u32[]{:S(2)}, u32[]{:S(2)}) %collective-permute-start) | collective-permute-done | bytes 12320 | tf_op jit(solution)/shard_map/ppermute | solution.py:298
  41.7 0.0 copy-done.1
  41.7 0.0 copy-done
  41.8 0.0 copy-done.2
  41.8 4.9 %shard_map.47 = bf16[16,16,2048]{2,1,0:T(8,128)(2,1)} custom-call(s32[1]{0:T(128)} %bitcast.tile_row_ref, s32[17]{0:T(128)S(1)} %copy-done.2, s32[4,32]{1,0:T(4,128)S(1)} %copy-done, s32[4,32]{1,0:T(4,128)S(1)} %copy-done.1, f32[24,128]{1,0:T(8,128)S(1)} %shard_map.46.refs_0_, f32[24,128]{1,0:T(8,128)S(1)} %collective-permute-done.refs_1_, ...), custom_call_target="tpu_custom_call" | custom-call | flops 16777216 | bytes 2097152 | tf_op jit(solution)/shard_map/pallas_call | solution.py:303
Async XLA Ops:
  36.0 4.7 %collective-permute-start.2 = (f32[24,128]{1,0:T(8,128)S(1)}, f32[24,128]{1,0:T(8,128)S(1)}, u32[]{:S(2)}, u32[]{:S(2)}) collective-permute-start(f32[24,128]{1,0:T(8,128)S(1)} %shard_map.46.refs_0_), channel_id=1, source_target_pairs={{0,6},{2,4},{4,2},{6,0},{8,14},{10,12},{12,10},{14,8},{16,22},{18,... | collective-permute-start | bytes 36872 | tf_op jit(solution)/shard_map/ppermute | solution.py:298
  36.9 3.8 %collective-permute-start.1 = (f32[24,128]{1,0:T(8,128)S(1)}, f32[24,128]{1,0:T(8,128)S(1)}, u32[]{:S(2)}, u32[]{:S(2)}) collective-permute-start(f32[24,128]{1,0:T(8,128)S(1)} %shard_map.46.refs_0_), channel_id=1, source_target_pairs={{0,4},{2,6},{4,0},{6,2},{8,12},{10,14},{12,8},{14,10},{16,20},{18,... | collective-permute-start | bytes 36872 | tf_op jit(solution)/shard_map/ppermute | solution.py:298
  38.1 3.7 %collective-permute-start = (f32[24,128]{1,0:T(8,128)S(1)}, f32[24,128]{1,0:T(8,128)S(1)}, u32[]{:S(2)}, u32[]{:S(2)}) collective-permute-start(f32[24,128]{1,0:T(8,128)S(1)} %shard_map.46.refs_0_), channel_id=1, source_target_pairs={{0,2},{2,0},{4,6},{6,4},{8,10},{10,8},{12,14},{14,12},{16,18},{18,... | collective-permute-start | bytes 36872 | tf_op jit(solution)/shard_map/ppermute | solution.py:298
  39.5 2.2 %copy-start.1 = (s32[4,32]{1,0:T(4,128)S(1)}, s32[4,32]{1,0:T(4,128)}, u32[]{:S(2)}) copy-start(s32[4,32]{1,0:T(4,128)} %step_ref.1) | copy-start | bytes 1540
  39.5 2.2 %copy-start = (s32[4,32]{1,0:T(4,128)S(1)}, s32[4,32]{1,0:T(4,128)}, u32[]{:S(2)}) copy-start(s32[4,32]{1,0:T(4,128)} %offset_ref.1) | copy-start | bytes 1540
  39.5 2.2 %copy-start.2 = (s32[17]{0:T(128)S(1)}, s32[17]{0:T(128)}, u32[]{:S(2)}) copy-start(s32[17]{0:T(128)} %knots_ref.1) | copy-start | bytes 208

commit v2 on v1

--- a/solution.py
+++ b/solution.py
@@ -153,11 +153,39 @@
     return dot(high, ones) + (dot(middle, ones) + dot(low, ones))
 
 
-def sums_kernel(x_ref, sums_ref, pairs_ref, totals_ref):
+def tables_kernel(
+    tile_row_ref,
+    knots_ref,
+    offset_ref,
+    step_ref,
+    pairing_ref,
+    of_tile_ref,
+    to_pixels_ref,
+    fraction_ref,
+    curve_ref,
+):
+    pairing_ref[...] = one_hot(pairing_ref.shape, lambda r: r // 2, lambda c: c)
+    of_tile_ref[...] = one_hot(
+        of_tile_ref.shape, lambda r: r // (TILE // 2), lambda c: c
+    )
+    to_pixels_ref[...] = one_hot(to_pixels_ref.shape, lambda r: r, lambda c: c // TILE)
+    outputs = fraction_ref.shape[0]
+    row = tile_row_ref[0]
+    offset = offset_ref[pl.ds(row, 1), :]
+    step = step_ref[pl.ds(row, 1), :]
+    index = lax.broadcasted_iota(jnp.int32, fraction_ref.shape, 0)
+    fraction_ref[...] = (offset + index * step).astype(jnp.float32) / (64.0 * outputs)
+    for j in range(curve_ref.shape[0]):
+        curve_ref[pl.ds(j, 1), :] = jnp.full(
+            (1, curve_ref.shape[1]), knots_ref[j].astype(jnp.float32) / 1000.0
+        )
+
+
+def sums_kernel(x_ref, pairing_ref, of_tile_ref, sums_ref, pairs_ref, totals_ref):
     sections, rows, cols = x_ref.shape
     half = cols // 2
     tiles = cols // TILE
-    pairing = one_hot((2 * LANES, LANES), lambda r: r // 2, lambda c: c)
+    pairing = pairing_ref[...]
     for g in range(half // LANES):
         wide = x_ref[:, :, 2 * LANES * g : 2 * LANES * (g + 1)]
         pairs_ref[g] = jnp.dot(
@@ -177,18 +205,16 @@
                 totals[k + 1] = totals[k + 1] + reduced * shift_up(reduced, k)
         for q in range(AHEAD + 2):
             totals_ref[sections * q : sections * (q + 1), lanes] = totals[q]
-    of_tile = one_hot((half, tiles), lambda r: r // (TILE // 2), lambda c: c)
-    sums = split_dot(totals_ref[...], of_tile)
+    sums = split_dot(totals_ref[...], of_tile_ref[...])
     wide = LANES // tiles
     height = sums.shape[0] // wide
     for q in range(wide):
         sums_ref[:, tiles * q : tiles * (q + 1)] = sums[height * q : height * (q + 1)]
 
 
-def resample_kernel(
-    tile_row_ref, knots_ref, offset_ref, step_ref, *refs
-):
-    *sums_refs, x_ref, out_ref, weights_ref, spread_ref = refs
+def resample_kernel(fraction_ref, curve_ref, to_pixels_ref, *refs):
+    *sums_refs, x_ref, out_ref, bracket_ref, place_ref, spread_ref, made_ref = refs[:-2]
+    place_sem, out_sems = refs[-2:]
     sections, rows, cols = x_ref.shape
     outputs = out_ref.shape[0]
     tiles = cols // TILE
@@ -206,7 +232,7 @@
     place = lax.broadcasted_iota(jnp.int32, (sections, tiles), 0)
     numerator = jnp.zeros((sections, tiles), jnp.float32)
     denominator = jnp.zeros((sections, tiles), jnp.float32)
-    knots = knots_ref.shape[0]
+    knots = curve_ref.shape[0]
     for k in range(1, AHEAD + 1):
         covariance = quantity[k + 1] / samples - mean * shift_up(mean, k)
         correlation = covariance / jnp.sqrt(variance * shift_up(variance, k) + EPSILON)
@@ -214,7 +240,7 @@
         for j in range(knots):
             grid = -1.0 + j * (2.0 / (knots - 1))
             hat = jnp.maximum(0.0, 1.0 - jnp.abs(correlation - grid) * ((knots - 1) / 2.0))
-            distance = distance + hat * (knots_ref[j].astype(jnp.float32) / 1000.0)
+            distance = distance + hat * curve_ref[j : j + 1, :]
         usable = (place + k < sections).astype(jnp.float32)
         numerator = numerator + usable * (k * distance)
         denominator = denominator + usable * float(k * k)
@@ -222,12 +248,7 @@
     depths = [jnp.zeros((1, tiles), jnp.float32)]
     for s in range(sections - 1):
         depths.append(depths[-1] + thickness[s : s + 1])
-    row = tile_row_ref[0]
-    offset = offset_ref[pl.ds(row, 1), :]
-    step = step_ref[pl.ds(row, 1), :]
-    index = lax.broadcasted_iota(jnp.int32, (outputs, tiles), 0)
-    fraction = (offset + index * step).astype(jnp.float32) / (64.0 * outputs)
-    target = depths[-1] * fraction
+    target = depths[-1] * fraction_ref[...]
     bracket = jnp.zeros((outputs, tiles), jnp.int32)
     for s in range(1, sections):
         bracket = bracket + (depths[s] <= target).astype(jnp.int32)
@@ -239,24 +260,41 @@
         lower = jnp.where(here, depths[s], lower)
         upper = jnp.where(here, depths[s + 1], upper)
     lifted = bracket.astype(jnp.float32) + (target - lower) / (upper - lower)
-    for s in range(sections):
-        weights_ref[outputs * s : outputs * (s + 1), :] = jnp.maximum(
-            0.0, 1.0 - jnp.abs(lifted - float(s))
-        ).astype(jnp.bfloat16)
-    to_pixels = one_hot((tiles, cols), lambda r: r, lambda c: c // TILE)
+    bracket_ref[:, :tiles] = bracket
+    to_smem = pltpu.make_async_copy(bracket_ref, place_ref, place_sem)
+    to_smem.start()
+    beyond = lifted - bracket.astype(jnp.float32)
+    pair = jnp.concatenate(
+        [1.0 - jnp.abs(beyond), jnp.maximum(0.0, 1.0 - jnp.abs(beyond - 1.0))], axis=0
+    )
     spread_ref[...] = jnp.dot(
-        weights_ref[...], to_pixels, preferred_element_type=jnp.float32
-    )
-
-    @pl.loop(0, cols // LANES)
-    def _(g):
-        lanes = pl.ds(pl.multiple_of(g * LANES, LANES), LANES)
-        pixels = [x_ref[s, :, lanes].astype(jnp.float32) for s in range(sections)]
-        for j in range(outputs):
-            total = jnp.zeros((rows, LANES), jnp.float32)
-            for s in range(sections):
-                total = total + spread_ref[pl.ds(outputs * s + j, 1), lanes] * pixels[s]
-            out_ref[j, :, lanes] = total.astype(jnp.bfloat16)
+        jnp.maximum(0.0, pair).astype(jnp.bfloat16),
+        to_pixels_ref[...],
+        preferred_element_type=jnp.float32,
+    )
+    to_smem.wait()
+    first = lax.broadcasted_iota(jnp.int32, (rows, LANES), 1) < TILE
+
+    def to_hbm(j):
+        return pltpu.make_async_copy(made_ref.at[j], out_ref.at[j], out_sems.at[j])
+
+    for j in range(outputs):
+        for g in range(cols // LANES):
+            lanes = pl.ds(g * LANES, LANES)
+            left = place_ref[j, 2 * g]
+            right = place_ref[j, 2 * g + 1]
+            near = jnp.where(first, x_ref[left, :, lanes], x_ref[right, :, lanes])
+            far = jnp.where(
+                first, x_ref[left + 1, :, lanes], x_ref[right + 1, :, lanes]
+            )
+            made_ref[j, :, lanes] = (
+                spread_ref[pl.ds(j, 1), lanes] * near.astype(jnp.float32)
+                + spread_ref[pl.ds(outputs + j, 1), lanes] * far.astype(jnp.float32)
+            ).astype(jnp.bfloat16)
+        to_hbm(j).start()
+
+    for j in range(outputs):
+        to_hbm(j).wait()
 
 
 def per_device(sections, calibration_knots, target_offset, target_step):
@@ -276,10 +314,27 @@
     vmem = pl.BlockSpec(memory_space=pltpu.VMEM)
     smem = pl.BlockSpec(memory_space=pltpu.SMEM)
     pixels = section_total * rows_local * cols
+    tile_row = (position * rows_local // TILE).astype(jnp.int32).reshape(1)
+    pairing, of_tile, to_pixels, fraction, curve = pl.pallas_call(
+        tables_kernel,
+        out_shape=[
+            jax.ShapeDtypeStruct((2 * LANES, LANES), jnp.bfloat16),
+            jax.ShapeDtypeStruct((cols // 2, tiles), jnp.bfloat16),
+            jax.ShapeDtypeStruct((tiles, cols), jnp.bfloat16),
+            jax.ShapeDtypeStruct((section_total, tiles), jnp.float32),
+            jax.ShapeDtypeStruct((calibration_knots.shape[0], tiles), jnp.float32),
+        ],
+        in_specs=[smem, smem, vmem, vmem],
+        out_specs=[vmem] * 5,
+        compiler_params=pltpu.CompilerParams(vmem_limit_bytes=4 * 2**20),
+        cost_estimate=pl.CostEstimate(
+            flops=2**20, bytes_accessed=2**20, transcendentals=0
+        ),
+    )(tile_row, calibration_knots, target_offset, target_step)
     partial_sums = pl.pallas_call(
         sums_kernel,
         out_shape=jax.ShapeDtypeStruct((height, LANES), jnp.float32),
-        in_specs=[vmem],
+        in_specs=[vmem] * 3,
         out_specs=vmem,
         scratch_shapes=[
             pltpu.VMEM(
@@ -287,11 +342,11 @@
             ),
             pltpu.VMEM(((AHEAD + 2) * section_total, cols // 2), jnp.float32),
         ],
-        compiler_params=pltpu.CompilerParams(vmem_limit_bytes=32 * 2**20),
+        compiler_params=pltpu.CompilerParams(vmem_limit_bytes=16 * 2**20),
         cost_estimate=pl.CostEstimate(
             flops=pixels * 8, bytes_accessed=pixels * 2, transcendentals=0
         ),
-    )(pencils)
+    )(pencils, pairing, of_tile)
     all_sums = [partial_sums]
     for other in range(1, sharers):
         all_sums.append(
@@ -299,21 +354,24 @@
                 partial_sums, "sec", [(i, i ^ other) for i in range(section_total)]
             )
         )
-    tile_row = (position * rows_local // TILE).astype(jnp.int32).reshape(1)
     return pl.pallas_call(
         resample_kernel,
         out_shape=jax.ShapeDtypeStruct(pencils.shape, jnp.bfloat16),
-        in_specs=[smem, smem, vmem, vmem] + [vmem] * sharers + [vmem],
-        out_specs=vmem,
+        in_specs=[vmem] * (sharers + 4),
+        out_specs=pl.BlockSpec(memory_space=pl.ANY),
         scratch_shapes=[
-            pltpu.VMEM((section_total * section_total, tiles), jnp.bfloat16),
-            pltpu.VMEM((section_total * section_total, cols), jnp.float32),
+            pltpu.VMEM((section_total, LANES), jnp.int32),
+            pltpu.SMEM((section_total, LANES), jnp.int32),
+            pltpu.VMEM((2 * section_total, cols), jnp.float32),
+            pltpu.VMEM(pencils.shape, jnp.bfloat16),
+            pltpu.SemaphoreType.DMA,
+            pltpu.SemaphoreType.DMA((section_total,)),
         ],
-        compiler_params=pltpu.CompilerParams(vmem_limit_bytes=32 * 2**20),
+        compiler_params=pltpu.CompilerParams(vmem_limit_bytes=16 * 2**20),
         cost_estimate=pl.CostEstimate(
             flops=pixels * 2 * section_total, bytes_accessed=pixels * 4, transcendentals=0
         ),
-    )(tile_row, calibration_knots, target_offset, target_step, *all_sums, pencils)
+    )(fraction, curve, to_pixels, *all_sums, pencils)
 
 
 def solution(mesh):

time: 46.9 us -> 42.4 us (0.904)
  blocking collectives: 34.7 us -> 0 us
  waiting for transfers between devices: 2.22 us -> 25.3 us
  starting transfers between devices: 3.55 us -> 11.9 us
  Pallas kernels: 6.22 us -> 4.3 us
  local copies, waits for them, and re-layouts: 0.01 us -> 0.67 us
    all_to_all x1 -> x0, blocking collectives: 34.7 us -> none  [per_device(): lax.all_to_all(blocks, 'sec', split_axis=0, concat_axis=0, tiled=True)]
    all_to_all x0 -> x1, waiting for transfers between devices: none -> 23.1 us  [per_device(): lax.all_to_all(blocks, 'sec', split_axis=0, concat_axis=0, tiled=True)]
    all_to_all x0 -> x1, starting transfers between devices: none -> 8.31 us  [per_device(): lax.all_to_all(blocks, 'sec', split_axis=0, concat_axis=0, tiled=True)]
    pallas_call x1, Pallas kernels: 4.94 us -> 2.39 us  [per_device(): pl.pallas_call(resample_kernel, out_shape=jax.ShapeDtypeStruct(pencils.sh...]
    pallas_call x0 -> x1, Pallas kernels: none -> 0.66 us  [per_device(): pl.pallas_call(tables_kernel, out_shape=[jax.ShapeDtypeStruct((2 * LANES,...]
    unnamed x6, local copies, waits for them, and re-layouts: 0.01 us -> 0.67 us
  transfers between devices with their start and end apart: 3 -> 4, of which waited for: 3 -> 4; matrix products, arithmetic and copies ran while one was open for 0% -> 0% of each run, Pallas kernels for 0% -> 2%
where the time goes in v2:
time: 42.4 us; the launch traced here: 42.2 us
  waiting for transfers between devices  25.3 us (60%)
  starting transfers between devices  11.9 us (28%)
  Pallas kernels  4.3 us (10%)
  local copies, waits for them, and re-layouts  0.67 us (2%)
    all_to_all x1, waiting for transfers between devices, per_device(): lax.all_to_all(blocks, 'sec', split_axis=0, concat_axis=0, tiled=True)  23.1 us
    all_to_all x1, starting transfers between devices, per_device(): lax.all_to_all(blocks, 'sec', split_axis=0, concat_axis=0, tiled=True)  8.31 us
    ppermute x3, starting transfers between devices, per_device(): lax.ppermute(partial_sums, 'sec', [(i, i ^ other) for i in range(section_...  3.55 us
    pallas_call x1, Pallas kernels, per_device(): pl.pallas_call(resample_kernel, out_shape=jax.ShapeDtypeStruct(pencils.sh...  2.39 us
    ppermute x3, waiting for transfers between devices, per_device(): lax.ppermute(partial_sums, 'sec', [(i, i ^ other) for i in range(section_...  2.25 us
    pallas_call x1, Pallas kernels, per_device(): pl.pallas_call(sums_kernel, out_shape=jax.ShapeDtypeStruct((height, LANES...  1.25 us
  transfers between devices with their start and end apart: 4, of which 4 were waited for; matrix products, arithmetic and copies ran while one was open for 0% of the time, Pallas kernels for 2%

profile of v2, /device:TPU:0, one launch (start us, length us, event | category | flops | bytes accessed | tf_op | source)
XLA Modules:
  0.0 42.2 jit_solution(465617701079271959)
XLA Ops:
  0.0 8.3 %all-to-all-start = ((bf16[16,16,2048]{2,1,0:T(8,128)(2,1)}), bf16[16,16,2048]{2,1,0:T(8,128)(2,1)S(1)}, u32[]{:S(2)}, u32[]{:S(2)}) async-start(bf16[16,16,2048]{2,1,0:T(8,128)(2,1)} %bitcast.2), calls=%async_computation | async-start | bytes 2097152 | tf_op jit(solution)/shard_map/all_to_all | solution.py:312
  8.3 0.0 copy-start.1
  8.3 0.0 copy-start
  8.4 0.0 copy-start.2
  8.4 0.6 %copy-done.1 = s32[4,32]{1,0:T(4,128)S(1)} copy-done((s32[4,32]{1,0:T(4,128)S(1)}, s32[4,32]{1,0:T(4,128)}, u32[]{:S(2)}) %copy-start.1) | copy-done | bytes 536
  9.0 0.0 copy-done
  9.0 0.0 copy-done.2
  9.0 0.7 %shard_map.46 = (bf16[256,128]{1,0:T(8,128)(2,1)S(1)}, bf16[1024,32]{1,0:T(8,128)(2,1)S(1)}, bf16[32,2048]{1,0:T(8,128)(2,1)S(1)}, f32[16,32]{1,0:T(8,128)S(1)}, f32[17,32]{1,0:T(8,128)S(1)}) custom-call(s32[1]{0:T(128)} %bitcast.tile_row_ref, s32[17]{0:T(128)S(1)} %copy-done.2, s32[4,32]{1,0:T(4,128)S(1)} %copy-done, s32[4,32]{1,0:T(4,128)S(1)} %copy-done.1), custom_call_target="tpu_custom_call" | custom-call | flops 1048576 | bytes 1048576 | tf_op jit(solution)/shard_map/pallas_call | solution.py:318
  9.7 23.1 %all-to-all-done.x_ref.refs_4_ = bf16[16,16,2048]{2,1,0:T(8,128)(2,1)S(1)} async-done(((bf16[16,16,2048]{2,1,0:T(8,128)(2,1)}), bf16[16,16,2048]{2,1,0:T(8,128)(2,1)S(1)}, u32[]{:S(2)}, u32[]{:S(2)}) %all-to-all-start) | async-done | bytes 1048608 | tf_op jit(solution)/shard_map/all_to_all | solution.py:312
  32.8 1.2 %shard_map.47.refs_0_ = f32[24,128]{1,0:T(8,128)S(1)} custom-call(bf16[16,16,2048]{2,1,0:T(8,128)(2,1)S(1)} %all-to-all-done.x_ref.refs_4_, bf16[256,128]{1,0:T(8,128)(2,1)S(1)} %get-tuple-element.13.pairing_ref, bf16[1024,32]{1,0:T(8,128)(2,1)S(1)} %get-tuple-element.14.of_tile_ref), custom_call_target="tpu_custom_call" | custom-call | flops 4194304 | bytes 1048576 | tf_op jit(solution)/shard_map/pallas_call | solution.py:334
  34.0 2.0 %collective-permute-start.2 = (f32[24,128]{1,0:T(8,128)S(1)}, f32[24,128]{1,0:T(8,128)S(1)}, u32[]{:S(2)}, u32[]{:S(2)}) collective-permute-start(f32[24,128]{1,0:T(8,128)S(1)} %shard_map.47.refs_0_), channel_id=1, source_target_pairs={{0,6},{2,4},{4,2},{6,0},{8,14},{10,12},{12,10},{14,8},{16,22},{18,... | collective-permute-start | bytes 36872 | tf_op jit(solution)/shard_map/ppermute | solution.py:353
  36.0 0.1 collective-permute-start.1
  36.1 1.4 %collective-permute-start = (f32[24,128]{1,0:T(8,128)S(1)}, f32[24,128]{1,0:T(8,128)S(1)}, u32[]{:S(2)}, u32[]{:S(2)}) collective-permute-start(f32[24,128]{1,0:T(8,128)S(1)} %shard_map.47.refs_0_), channel_id=1, source_target_pairs={{0,2},{2,0},{4,6},{6,4},{8,10},{10,8},{12,14},{14,12},{16,18},{18,... | collective-permute-start | bytes 36872 | tf_op jit(solution)/shard_map/ppermute | solution.py:353
  37.6 1.1 %collective-permute-done.2.refs_3_ = f32[24,128]{1,0:T(8,128)S(1)} collective-permute-done((f32[24,128]{1,0:T(8,128)S(1)}, f32[24,128]{1,0:T(8,128)S(1)}, u32[]{:S(2)}, u32[]{:S(2)}) %collective-permute-start.2) | collective-permute-done | bytes 12320 | tf_op jit(solution)/shard_map/ppermute | solution.py:353
  38.7 1.1 %collective-permute-done.1.refs_2_ = f32[24,128]{1,0:T(8,128)S(1)} collective-permute-done((f32[24,128]{1,0:T(8,128)S(1)}, f32[24,128]{1,0:T(8,128)S(1)}, u32[]{:S(2)}, u32[]{:S(2)}) %collective-permute-start.1) | collective-permute-done | bytes 12320 | tf_op jit(solution)/shard_map/ppermute | solution.py:353
  39.7 0.1 collective-permute-done.refs_1_
  39.8 2.4 %shard_map.48 = bf16[16,16,2048]{2,1,0:T(8,128)(2,1)} custom-call(f32[16,32]{1,0:T(8,128)S(1)} %get-tuple-element.10.fraction_ref, f32[17,32]{1,0:T(8,128)S(1)} %get-tuple-element.11.curve_ref, bf16[32,2048]{1,0:T(8,128)(2,1)S(1)} %get-tuple-element.12.to_pixels_ref, f32[24,128]{1,0:T(8,128)S(1)} %shard_map.47.refs_0_, ...), custom_call_target="tpu_custom_call" | custom-call | flops 16777216 | bytes 2097152 | tf_op jit(solution)/shard_map/pallas_call | solution.py:357
Async XLA Ops:
  0.0 32.8 %all-to-all-start = ((bf16[16,16,2048]{2,1,0:T(8,128)(2,1)}), bf16[16,16,2048]{2,1,0:T(8,128)(2,1)S(1)}, u32[]{:S(2)}, u32[]{:S(2)}) async-start(bf16[16,16,2048]{2,1,0:T(8,128)(2,1)} %bitcast.2), calls=%async_computation | async-start | bytes 2097152 | tf_op jit(solution)/shard_map/all_to_all | solution.py:312
  8.3 0.7 %copy-start.1 = (s32[4,32]{1,0:T(4,128)S(1)}, s32[4,32]{1,0:T(4,128)}, u32[]{:S(2)}) copy-start(s32[4,32]{1,0:T(4,128)} %step_ref.1) | copy-start | bytes 1540
  8.3 0.7 %copy-start = (s32[4,32]{1,0:T(4,128)S(1)}, s32[4,32]{1,0:T(4,128)}, u32[]{:S(2)}) copy-start(s32[4,32]{1,0:T(4,128)} %offset_ref.1) | copy-start | bytes 1540
  8.4 0.7 %copy-start.2 = (s32[17]{0:T(128)S(1)}, s32[17]{0:T(128)}, u32[]{:S(2)}) copy-start(s32[17]{0:T(128)} %knots_ref.1) | copy-start | bytes 208
  34.0 4.7 %collective-permute-start.2 = (f32[24,128]{1,0:T(8,128)S(1)}, f32[24,128]{1,0:T(8,128)S(1)}, u32[]{:S(2)}, u32[]{:S(2)}) collective-permute-start(f32[24,128]{1,0:T(8,128)S(1)} %shard_map.47.refs_0_), channel_id=1, source_target_pairs={{0,6},{2,4},{4,2},{6,0},{8,14},{10,12},{12,10},{14,8},{16,22},{18,... | collective-permute-start | bytes 36872 | tf_op jit(solution)/shard_map/ppermute | solution.py:353
  36.0 3.7 %collective-permute-start.1 = (f32[24,128]{1,0:T(8,128)S(1)}, f32[24,128]{1,0:T(8,128)S(1)}, u32[]{:S(2)}, u32[]{:S(2)}) collective-permute-start(f32[24,128]{1,0:T(8,128)S(1)} %shard_map.47.refs_0_), channel_id=1, source_target_pairs={{0,4},{2,6},{4,0},{6,2},{8,12},{10,14},{12,8},{14,10},{16,20},{18,... | collective-permute-start | bytes 36872 | tf_op jit(solution)/shard_map/ppermute | solution.py:353
  36.1 3.7 %collective-permute-start = (f32[24,128]{1,0:T(8,128)S(1)}, f32[24,128]{1,0:T(8,128)S(1)}, u32[]{:S(2)}, u32[]{:S(2)}) collective-permute-start(f32[24,128]{1,0:T(8,128)S(1)} %shard_map.47.refs_0_), channel_id=1, source_target_pairs={{0,2},{2,0},{4,6},{6,4},{8,10},{10,8},{12,14},{14,12},{16,18},{18,... | collective-permute-start | bytes 36872 | tf_op jit(solution)/shard_map/ppermute | solution.py:353

commit v3 on v2

--- a/solution.py
+++ b/solution.py
@@ -144,13 +144,14 @@
     return jnp.concatenate([values[steps:], jnp.zeros_like(values[:steps])], axis=0)
 
 
-def split_dot(values, ones):
-    high = values.astype(jnp.bfloat16)
-    rest = values - high.astype(jnp.float32)
-    middle = rest.astype(jnp.bfloat16)
-    low = (rest - middle.astype(jnp.float32)).astype(jnp.bfloat16)
-    dot = functools.partial(jnp.dot, preferred_element_type=jnp.float32)
-    return dot(high, ones) + (dot(middle, ones) + dot(low, ones))
+def tile_of_lane(lanes):
+    group = (lanes // 16) % 2 + 2 * ((lanes // 8) % 2) + 4 * ((lanes // 4) % 2)
+    return lanes // 32 + 4 * group
+
+
+def lane_of_tile(tile):
+    group = tile // 4
+    return 32 * (tile % 4) + 16 * (group % 2) + 8 * (group // 2 % 2) + 4 * (group // 4)
 
 
 def tables_kernel(
@@ -159,74 +160,104 @@
     offset_ref,
     step_ref,
     pairing_ref,
-    of_tile_ref,
     to_pixels_ref,
     fraction_ref,
     curve_ref,
 ):
     pairing_ref[...] = one_hot(pairing_ref.shape, lambda r: r // 2, lambda c: c)
-    of_tile_ref[...] = one_hot(
-        of_tile_ref.shape, lambda r: r // (TILE // 2), lambda c: c
-    )
-    to_pixels_ref[...] = one_hot(to_pixels_ref.shape, lambda r: r, lambda c: c // TILE)
+    to_pixels_ref[...] = one_hot(
+        to_pixels_ref.shape,
+        lambda r: jnp.where(r % 4 == 0, tile_of_lane(r), -1),
+        lambda c: c // TILE,
+    )
     outputs = fraction_ref.shape[0]
     row = tile_row_ref[0]
-    offset = offset_ref[pl.ds(row, 1), :]
-    step = step_ref[pl.ds(row, 1), :]
-    index = lax.broadcasted_iota(jnp.int32, fraction_ref.shape, 0)
-    fraction_ref[...] = (offset + index * step).astype(jnp.float32) / (64.0 * outputs)
+    to_lanes = one_hot(
+        (offset_ref.shape[1], LANES), lambda r: r, lambda c: tile_of_lane(c)
+    )
+
+    def spread(ref):
+        values = jnp.broadcast_to(ref[pl.ds(row, 1), :], (16, ref.shape[1]))
+        return jnp.dot(
+            values.astype(jnp.float32).astype(jnp.bfloat16),
+            to_lanes,
+            preferred_element_type=jnp.float32,
+        )[:1]
+
+    index = lax.broadcasted_iota(jnp.int32, fraction_ref.shape, 0).astype(jnp.float32)
+    fraction_ref[...] = (spread(offset_ref) + index * spread(step_ref)) / (
+        64.0 * outputs
+    )
     for j in range(curve_ref.shape[0]):
         curve_ref[pl.ds(j, 1), :] = jnp.full(
             (1, curve_ref.shape[1]), knots_ref[j].astype(jnp.float32) / 1000.0
         )
 
 
-def sums_kernel(x_ref, pairing_ref, of_tile_ref, sums_ref, pairs_ref, totals_ref):
+def fold(first, second, width, lanes):
+    return jnp.where(
+        (lanes // width) % 2 == 0,
+        first + pltpu.roll(first, LANES - width, 1),
+        second + pltpu.roll(second, width, 1),
+    )
+
+
+def sums_kernel(x_ref, pairing_ref, sums_ref, pairs_ref, reduced_ref):
     sections, rows, cols = x_ref.shape
-    half = cols // 2
-    tiles = cols // TILE
+    groups = cols // 2 // LANES
     pairing = pairing_ref[...]
-    for g in range(half // LANES):
+    for g in range(groups):
         wide = x_ref[:, :, 2 * LANES * g : 2 * LANES * (g + 1)]
-        pairs_ref[g] = jnp.dot(
+        pairs = jnp.dot(
             wide.reshape(sections * rows, 2 * LANES),
             pairing,
             preferred_element_type=jnp.float32,
         )
-    for g in range(half // LANES):
-        lanes = pl.ds(LANES * g, LANES)
-        totals = [jnp.zeros((sections, LANES), jnp.float32)] * (AHEAD + 2)
+        for s in range(sections):
+            pairs_ref[g, pl.ds(17 * s, rows), :] = pairs[rows * s : rows * (s + 1)]
+    lanes = lax.broadcasted_iota(jnp.int32, (sections, LANES), 1)
+    waiting = {}
+    for g in range(groups):
+        total = [jnp.zeros((sections, LANES), jnp.float32)] * (AHEAD + 2)
         for r in range(rows // 2):
-            upper = pairs_ref[g, pl.ds(2 * r, sections, stride=rows), :]
-            lower = pairs_ref[g, pl.ds(2 * r + 1, sections, stride=rows), :]
+            upper = pairs_ref[g, pl.ds(2 * r, sections, stride=17), :]
+            lower = pairs_ref[g, pl.ds(2 * r + 1, sections, stride=17), :]
             reduced = ((upper + lower) * 0.25).astype(jnp.bfloat16).astype(jnp.float32)
-            totals[0] = totals[0] + reduced
-            for k in range(AHEAD + 1):
-                totals[k + 1] = totals[k + 1] + reduced * shift_up(reduced, k)
-        for q in range(AHEAD + 2):
-            totals_ref[sections * q : sections * (q + 1), lanes] = totals[q]
-    sums = split_dot(totals_ref[...], of_tile_ref[...])
-    wide = LANES // tiles
-    height = sums.shape[0] // wide
-    for q in range(wide):
-        sums_ref[:, tiles * q : tiles * (q + 1)] = sums[height * q : height * (q + 1)]
+            reduced_ref[g, r, :sections] = reduced
+            reduced_ref[g, r, sections:] = jnp.zeros((8, LANES), jnp.float32)
+            total[0] = total[0] + reduced
+            total[1] = total[1] + reduced * reduced
+            for k in range(1, AHEAD + 1):
+                total[k + 1] = total[k + 1] + reduced * reduced_ref[g, r, k : k + sections]
+        width = 16
+        while (g * width // 16) % 2 == 1 and width >= 4:
+            total = [fold(a, b, width, lanes) for a, b in zip(waiting.pop(width), total)]
+            width //= 2
+        waiting[width] = total
+    total = waiting.pop(2)
+    for v in range((AHEAD + 2) // 2):
+        pair = fold(total[2 * v], total[2 * v + 1], 2, lanes)
+        sums_ref[8 * v : 8 * v + 8] = fold(pair[:8], pair[8:], 1, lanes[:8])
 
 
 def resample_kernel(fraction_ref, curve_ref, to_pixels_ref, *refs):
-    *sums_refs, x_ref, out_ref, bracket_ref, place_ref, spread_ref, made_ref = refs[:-2]
-    place_sem, out_sems = refs[-2:]
+    *sums_refs, x_ref, out_ref, spread_ref, made_ref, out_sems = refs
     sections, rows, cols = x_ref.shape
     outputs = out_ref.shape[0]
-    tiles = cols // TILE
+    tiles = LANES
     samples = float((TILE // 2) ** 2)
     packed = sums_refs[0][...]
     for ref in sums_refs[1:]:
         packed = packed + ref[...]
-    parts = LANES // tiles
-    sums = jnp.concatenate(
-        [packed[:, tiles * q : tiles * (q + 1)] for q in range(parts)], axis=0
-    )
-    quantity = [sums[sections * q : sections * (q + 1)] for q in range(AHEAD + 2)]
+
+    def unpack(q, half):
+        part = packed[8 * (q // 2) : 8 * (q // 2) + 8]
+        b = 2 * (q % 2) + half
+        return pltpu.roll(part, LANES - b, 1) if b else part
+
+    quantity = [
+        jnp.concatenate([unpack(q, 0), unpack(q, 1)], axis=0) for q in range(AHEAD + 2)
+    ]
     mean = quantity[0] / samples
     variance = quantity[1] / samples - mean * mean
     place = lax.broadcasted_iota(jnp.int32, (sections, tiles), 0)
@@ -260,19 +291,16 @@
         lower = jnp.where(here, depths[s], lower)
         upper = jnp.where(here, depths[s + 1], upper)
     lifted = bracket.astype(jnp.float32) + (target - lower) / (upper - lower)
-    bracket_ref[:, :tiles] = bracket
-    to_smem = pltpu.make_async_copy(bracket_ref, place_ref, place_sem)
-    to_smem.start()
     beyond = lifted - bracket.astype(jnp.float32)
     pair = jnp.concatenate(
         [1.0 - jnp.abs(beyond), jnp.maximum(0.0, 1.0 - jnp.abs(beyond - 1.0))], axis=0
     )
+    used = lax.broadcasted_iota(jnp.int32, pair.shape, 1) % 4 == 0
     spread_ref[...] = jnp.dot(
-        jnp.maximum(0.0, pair).astype(jnp.bfloat16),
+        jnp.where(used, jnp.maximum(0.0, pair), 0.0).astype(jnp.bfloat16),
         to_pixels_ref[...],
         preferred_element_type=jnp.float32,
     )
-    to_smem.wait()
     first = lax.broadcasted_iota(jnp.int32, (rows, LANES), 1) < TILE
 
     def to_hbm(j):
@@ -281,8 +309,8 @@
     for j in range(outputs):
         for g in range(cols // LANES):
             lanes = pl.ds(g * LANES, LANES)
-            left = place_ref[j, 2 * g]
-            right = place_ref[j, 2 * g + 1]
+            left = bracket[j, lane_of_tile(2 * g)]
+            right = bracket[j, lane_of_tile(2 * g + 1)]
             near = jnp.where(first, x_ref[left, :, lanes], x_ref[right, :, lanes])
             far = jnp.where(
                 first, x_ref[left + 1, :, lanes], x_ref[right + 1, :, lanes]
@@ -304,28 +332,27 @@
     rows_local = row_total // section_total
     sharers = TILE // rows_local
     tiles = cols // TILE
-    if rows_local % 16 or section_total % 8 or LANES % tiles or cols % (2 * LANES):
+    if rows_local % 16 or section_total != 16 or tiles * 4 != LANES or sharers > 16:
         return plain_per_device(
             sections, calibration_knots, target_offset, target_step
         )
     blocks = sections.reshape(section_total, rows_local, cols)
     pencils = lax.all_to_all(blocks, "sec", split_axis=0, concat_axis=0, tiled=True)
-    height = (AHEAD + 2) * section_total * tiles // LANES
+    height = 8 * (AHEAD + 2) // 2
     vmem = pl.BlockSpec(memory_space=pltpu.VMEM)
     smem = pl.BlockSpec(memory_space=pltpu.SMEM)
     pixels = section_total * rows_local * cols
     tile_row = (position * rows_local // TILE).astype(jnp.int32).reshape(1)
-    pairing, of_tile, to_pixels, fraction, curve = pl.pallas_call(
+    pairing, to_pixels, fraction, curve = pl.pallas_call(
         tables_kernel,
         out_shape=[
             jax.ShapeDtypeStruct((2 * LANES, LANES), jnp.bfloat16),
-            jax.ShapeDtypeStruct((cols // 2, tiles), jnp.bfloat16),
-            jax.ShapeDtypeStruct((tiles, cols), jnp.bfloat16),
-            jax.ShapeDtypeStruct((section_total, tiles), jnp.float32),
-            jax.ShapeDtypeStruct((calibration_knots.shape[0], tiles), jnp.float32),
+            jax.ShapeDtypeStruct((LANES, cols), jnp.bfloat16),
+            jax.ShapeDtypeStruct((section_total, LANES), jnp.float32),
+            jax.ShapeDtypeStruct((calibration_knots.shape[0], LANES), jnp.float32),
         ],
         in_specs=[smem, smem, vmem, vmem],
-        out_specs=[vmem] * 5,
+        out_specs=[vmem] * 4,
         compiler_params=pltpu.CompilerParams(vmem_limit_bytes=4 * 2**20),
         cost_estimate=pl.CostEstimate(
             flops=2**20, bytes_accessed=2**20, transcendentals=0
@@ -334,19 +361,22 @@
     partial_sums = pl.pallas_call(
         sums_kernel,
         out_shape=jax.ShapeDtypeStruct((height, LANES), jnp.float32),
-        in_specs=[vmem] * 3,
+        in_specs=[vmem] * 2,
         out_specs=vmem,
         scratch_shapes=[
             pltpu.VMEM(
-                (cols // 2 // LANES, section_total * rows_local, LANES), jnp.float32
+                (cols // 2 // LANES, section_total * 17, LANES), jnp.float32
             ),
-            pltpu.VMEM(((AHEAD + 2) * section_total, cols // 2), jnp.float32),
+            pltpu.VMEM(
+                (cols // 2 // LANES, rows_local // 2, section_total + 8, LANES),
+                jnp.float32,
+            ),
         ],
         compiler_params=pltpu.CompilerParams(vmem_limit_bytes=16 * 2**20),
         cost_estimate=pl.CostEstimate(
             flops=pixels * 8, bytes_accessed=pixels * 2, transcendentals=0
         ),
-    )(pencils, pairing, of_tile)
+    )(pencils, pairing)
     all_sums = [partial_sums]
     for other in range(1, sharers):
         all_sums.append(
@@ -360,11 +390,8 @@
         in_specs=[vmem] * (sharers + 4),
         out_specs=pl.BlockSpec(memory_space=pl.ANY),
         scratch_shapes=[
-            pltpu.VMEM((section_total, LANES), jnp.int32),
-            pltpu.SMEM((section_total, LANES), jnp.int32),
             pltpu.VMEM((2 * section_total, cols), jnp.float32),
             pltpu.VMEM(pencils.shape, jnp.bfloat16),
-            pltpu.SemaphoreType.DMA,
             pltpu.SemaphoreType.DMA((section_total,)),
         ],
         compiler_params=pltpu.CompilerParams(vmem_limit_bytes=16 * 2**20),

time: 42.4 us -> 41.5 us (0.979)
  Pallas kernels: 4.3 us -> 3.6 us
    pallas_call x1, Pallas kernels: 2.39 us -> 1.86 us  [per_device(): pl.pallas_call(resample_kernel, out_shape=jax.ShapeDtypeStruct(pencils.sh...]
where the time goes in v3:
time: 41.5 us; the launch traced here: 41.3 us
  waiting for transfers between devices  25.1 us (60%)
  starting transfers between devices  11.8 us (28%)
  Pallas kernels  3.6 us (9%)
  local copies, waits for them, and re-layouts  0.67 us (2%)
    all_to_all x1, waiting for transfers between devices, per_device(): lax.all_to_all(blocks, 'sec', split_axis=0, concat_axis=0, tiled=True)  22.9 us
    all_to_all x1, starting transfers between devices, per_device(): lax.all_to_all(blocks, 'sec', split_axis=0, concat_axis=0, tiled=True)  8.31 us
    ppermute x3, starting transfers between devices, per_device(): lax.ppermute(partial_sums, 'sec', [(i, i ^ other) for i in range(section_...  3.52 us
    ppermute x3, waiting for transfers between devices, per_device(): lax.ppermute(partial_sums, 'sec', [(i, i ^ other) for i in range(section_...  2.25 us
    pallas_call x1, Pallas kernels, per_device(): pl.pallas_call(resample_kernel, out_shape=jax.ShapeDtypeStruct(pencils.sh...  1.86 us
    pallas_call x1, Pallas kernels, per_device(): pl.pallas_call(sums_kernel, out_shape=jax.ShapeDtypeStruct((height, LANES...  0.88 us
    pallas_call x1, Pallas kernels, per_device(): pl.pallas_call(tables_kernel, out_shape=[jax.ShapeDtypeStruct((2 * LANES,...  0.86 us
  transfers between devices with their start and end apart: 4, of which 4 were waited for; matrix products, arithmetic and copies ran while one was open for 0% of the time, Pallas kernels for 2%

profile of v3, /device:TPU:0, one launch (start us, length us, event | category | flops | bytes accessed | tf_op | source)
XLA Modules:
  0.0 41.3 jit_solution(11997407621851464733)
XLA Ops:
  0.0 8.3 %all-to-all-start = ((bf16[16,16,2048]{2,1,0:T(8,128)(2,1)}), bf16[16,16,2048]{2,1,0:T(8,128)(2,1)S(1)}, u32[]{:S(2)}, u32[]{:S(2)}) async-start(bf16[16,16,2048]{2,1,0:T(8,128)(2,1)} %bitcast.2), calls=%async_computation | async-start | bytes 2097152 | tf_op jit(solution)/shard_map/all_to_all | solution.py:340
  8.3 0.0 copy-start.1
  8.3 0.0 copy-start
  8.4 0.0 copy-start.2
  8.4 0.6 %copy-done.1 = s32[4,32]{1,0:T(4,128)S(1)} copy-done((s32[4,32]{1,0:T(4,128)S(1)}, s32[4,32]{1,0:T(4,128)}, u32[]{:S(2)}) %copy-start.1) | copy-done | bytes 536
  9.0 0.0 copy-done
  9.0 0.0 copy-done.2
  9.0 0.9 %shard_map.46 = (bf16[256,128]{1,0:T(8,128)(2,1)S(1)}, bf16[128,2048]{1,0:T(8,128)(2,1)S(1)}, f32[16,128]{1,0:T(8,128)S(1)}, f32[17,128]{1,0:T(8,128)S(1)}) custom-call(s32[1]{0:T(128)} %bitcast.tile_row_ref, s32[17]{0:T(128)S(1)} %copy-done.2, s32[4,32]{1,0:T(4,128)S(1)} %copy-done, s32[4,32]{1,0:T(4,128)S(1)} %copy-done.1), custom_call_target="tpu_custom_call" | custom-call | flops 1048576 | bytes 1048576 | tf_op jit(solution)/shard_map/pallas_call | solution.py:346
  9.9 22.9 %all-to-all-done.x_ref.refs_4_ = bf16[16,16,2048]{2,1,0:T(8,128)(2,1)S(1)} async-done(((bf16[16,16,2048]{2,1,0:T(8,128)(2,1)}), bf16[16,16,2048]{2,1,0:T(8,128)(2,1)S(1)}, u32[]{:S(2)}, u32[]{:S(2)}) %all-to-all-start) | async-done | bytes 1048608 | tf_op jit(solution)/shard_map/all_to_all | solution.py:340
  32.8 0.9 %shard_map.47.refs_0_ = f32[24,128]{1,0:T(8,128)S(1)} custom-call(bf16[16,16,2048]{2,1,0:T(8,128)(2,1)S(1)} %all-to-all-done.x_ref.refs_4_, bf16[256,128]{1,0:T(8,128)(2,1)S(1)} %get-tuple-element.12.pairing_ref), custom_call_target="tpu_custom_call" | custom-call | flops 4194304 | bytes 1048576 | tf_op jit(solution)/shard_map/pallas_call | solution.py:361
  33.6 2.0 %collective-permute-start.2 = (f32[24,128]{1,0:T(8,128)S(1)}, f32[24,128]{1,0:T(8,128)S(1)}, u32[]{:S(2)}, u32[]{:S(2)}) collective-permute-start(f32[24,128]{1,0:T(8,128)S(1)} %shard_map.47.refs_0_), channel_id=1, source_target_pairs={{0,6},{2,4},{4,2},{6,0},{8,14},{10,12},{12,10},{14,8},{16,22},{18,... | collective-permute-start | bytes 36872 | tf_op jit(solution)/shard_map/ppermute | solution.py:383
  35.6 0.1 collective-permute-start.1
  35.7 1.4 %collective-permute-start = (f32[24,128]{1,0:T(8,128)S(1)}, f32[24,128]{1,0:T(8,128)S(1)}, u32[]{:S(2)}, u32[]{:S(2)}) collective-permute-start(f32[24,128]{1,0:T(8,128)S(1)} %shard_map.47.refs_0_), channel_id=1, source_target_pairs={{0,2},{2,0},{4,6},{6,4},{8,10},{10,8},{12,14},{14,12},{16,18},{18,... | collective-permute-start | bytes 36872 | tf_op jit(solution)/shard_map/ppermute | solution.py:383
  37.2 1.1 %collective-permute-done.2.refs_3_ = f32[24,128]{1,0:T(8,128)S(1)} collective-permute-done((f32[24,128]{1,0:T(8,128)S(1)}, f32[24,128]{1,0:T(8,128)S(1)}, u32[]{:S(2)}, u32[]{:S(2)}) %collective-permute-start.2) | collective-permute-done | bytes 12320 | tf_op jit(solution)/shard_map/ppermute | solution.py:383
  38.3 1.1 %collective-permute-done.1.refs_2_ = f32[24,128]{1,0:T(8,128)S(1)} collective-permute-done((f32[24,128]{1,0:T(8,128)S(1)}, f32[24,128]{1,0:T(8,128)S(1)}, u32[]{:S(2)}, u32[]{:S(2)}) %collective-permute-start.1) | collective-permute-done | bytes 12320 | tf_op jit(solution)/shard_map/ppermute | solution.py:383
  39.3 0.1 collective-permute-done.refs_1_
  39.4 1.9 %shard_map.48 = bf16[16,16,2048]{2,1,0:T(8,128)(2,1)} custom-call(f32[16,128]{1,0:T(8,128)S(1)} %get-tuple-element.9.fraction_ref, f32[17,128]{1,0:T(8,128)S(1)} %get-tuple-element.10.curve_ref, bf16[128,2048]{1,0:T(8,128)(2,1)S(1)} %get-tuple-element.11.to_pixels_ref, f32[24,128]{1,0:T(8,128)S(1)} %shard_map.47.refs_0_, ...), custom_call_target="tpu_custom_call" | custom-call | flops 16777216 | bytes 2097152 | tf_op jit(solution)/shard_map/pallas_call | solution.py:387
Async XLA Ops:
  0.0 32.8 %all-to-all-start = ((bf16[16,16,2048]{2,1,0:T(8,128)(2,1)}), bf16[16,16,2048]{2,1,0:T(8,128)(2,1)S(1)}, u32[]{:S(2)}, u32[]{:S(2)}) async-start(bf16[16,16,2048]{2,1,0:T(8,128)(2,1)} %bitcast.2), calls=%async_computation | async-start | bytes 2097152 | tf_op jit(solution)/shard_map/all_to_all | solution.py:340
  8.3 0.7 %copy-start.1 = (s32[4,32]{1,0:T(4,128)S(1)}, s32[4,32]{1,0:T(4,128)}, u32[]{:S(2)}) copy-start(s32[4,32]{1,0:T(4,128)} %step_ref.1) | copy-start | bytes 1540
  8.3 0.7 %copy-start = (s32[4,32]{1,0:T(4,128)S(1)}, s32[4,32]{1,0:T(4,128)}, u32[]{:S(2)}) copy-start(s32[4,32]{1,0:T(4,128)} %offset_ref.1) | copy-start | bytes 1540
  8.4 0.7 %copy-start.2 = (s32[17]{0:T(128)S(1)}, s32[17]{0:T(128)}, u32[]{:S(2)}) copy-start(s32[17]{0:T(128)} %knots_ref.1) | copy-start | bytes 208
  33.6 4.6 %collective-permute-start.2 = (f32[24,128]{1,0:T(8,128)S(1)}, f32[24,128]{1,0:T(8,128)S(1)}, u32[]{:S(2)}, u32[]{:S(2)}) collective-permute-start(f32[24,128]{1,0:T(8,128)S(1)} %shard_map.47.refs_0_), channel_id=1, source_target_pairs={{0,6},{2,4},{4,2},{6,0},{8,14},{10,12},{12,10},{14,8},{16,22},{18,... | collective-permute-start | bytes 36872 | tf_op jit(solution)/shard_map/ppermute | solution.py:383
  35.6 3.7 %collective-permute-start.1 = (f32[24,128]{1,0:T(8,128)S(1)}, f32[24,128]{1,0:T(8,128)S(1)}, u32[]{:S(2)}, u32[]{:S(2)}) collective-permute-start(f32[24,128]{1,0:T(8,128)S(1)} %shard_map.47.refs_0_), channel_id=1, source_target_pairs={{0,4},{2,6},{4,0},{6,2},{8,12},{10,14},{12,8},{14,10},{16,20},{18,... | collective-permute-start | bytes 36872 | tf_op jit(solution)/shard_map/ppermute | solution.py:383
  35.7 3.7 %collective-permute-start = (f32[24,128]{1,0:T(8,128)S(1)}, f32[24,128]{1,0:T(8,128)S(1)}, u32[]{:S(2)}, u32[]{:S(2)}) collective-permute-start(f32[24,128]{1,0:T(8,128)S(1)} %shard_map.47.refs_0_), channel_id=1, source_target_pairs={{0,2},{2,0},{4,6},{6,4},{8,10},{10,8},{12,14},{14,12},{16,18},{18,... | collective-permute-start | bytes 36872 | tf_op jit(solution)/shard_map/ppermute | solution.py:383

commit v4 on v3

--- a/solution.py
+++ b/solution.py
@@ -268,9 +268,9 @@
         covariance = quantity[k + 1] / samples - mean * shift_up(mean, k)
         correlation = covariance / jnp.sqrt(variance * shift_up(variance, k) + EPSILON)
         distance = jnp.zeros((sections, tiles), jnp.float32)
+        scaled = correlation * ((knots - 1) / 2.0)
         for j in range(knots):
-            grid = -1.0 + j * (2.0 / (knots - 1))
-            hat = jnp.maximum(0.0, 1.0 - jnp.abs(correlation - grid) * ((knots - 1) / 2.0))
+            hat = jnp.maximum(0.0, 1.0 - jnp.abs(scaled - (j - (knots - 1) / 2.0)))
             distance = distance + hat * curve_ref[j : j + 1, :]
         usable = (place + k < sections).astype(jnp.float32)
         numerator = numerator + usable * (k * distance)
@@ -304,24 +304,31 @@
     first = lax.broadcasted_iota(jnp.int32, (rows, LANES), 1) < TILE
 
     def to_hbm(j):
-        return pltpu.make_async_copy(made_ref.at[j], out_ref.at[j], out_sems.at[j])
+        some = pl.ds(2 * j, 2)
+        return pltpu.make_async_copy(
+            made_ref.at[some], out_ref.at[some], out_sems.at[j]
+        )
 
     for j in range(outputs):
+        made = []
         for g in range(cols // LANES):
             lanes = pl.ds(g * LANES, LANES)
-            left = bracket[j, lane_of_tile(2 * g)]
-            right = bracket[j, lane_of_tile(2 * g + 1)]
-            near = jnp.where(first, x_ref[left, :, lanes], x_ref[right, :, lanes])
-            far = jnp.where(
-                first, x_ref[left + 1, :, lanes], x_ref[right + 1, :, lanes]
+            ahead = x_ref[pl.ds(bracket[j, lane_of_tile(2 * g)], 2), :, lanes]
+            behind = x_ref[pl.ds(bracket[j, lane_of_tile(2 * g + 1)], 2), :, lanes]
+            near = jnp.where(first, ahead[0], behind[0])
+            far = jnp.where(first, ahead[1], behind[1])
+            made.append(
+                (
+                    spread_ref[j : j + 1, lanes] * near.astype(jnp.float32)
+                    + spread_ref[outputs + j : outputs + j + 1, lanes]
+                    * far.astype(jnp.float32)
+                ).astype(jnp.bfloat16)
             )
-            made_ref[j, :, lanes] = (
-                spread_ref[pl.ds(j, 1), lanes] * near.astype(jnp.float32)
-                + spread_ref[pl.ds(outputs + j, 1), lanes] * far.astype(jnp.float32)
-            ).astype(jnp.bfloat16)
-        to_hbm(j).start()
-
-    for j in range(outputs):
+        for g, values in enumerate(made):
+            made_ref[j, :, g * LANES : (g + 1) * LANES] = values
+        if j % 2:
+            to_hbm(j // 2).start()
+    for j in range(outputs // 2):
         to_hbm(j).wait()
 
 
@@ -392,7 +399,7 @@
         scratch_shapes=[
             pltpu.VMEM((2 * section_total, cols), jnp.float32),
             pltpu.VMEM(pencils.shape, jnp.bfloat16),
-            pltpu.SemaphoreType.DMA((section_total,)),
+            pltpu.SemaphoreType.DMA((section_total // 2,)),
         ],
         compiler_params=pltpu.CompilerParams(vmem_limit_bytes=16 * 2**20),
         cost_estimate=pl.CostEstimate(

time: 41.5 us -> 41.4 us (level)
  no operation moved by 1% of the time
where the time goes in v4:
time: 41.4 us; the launch traced here: 41.1 us
  waiting for transfers between devices  25.1 us (61%)
  starting transfers between devices  11.8 us (29%)
  Pallas kernels  3.47 us (8%)
  local copies, waits for them, and re-layouts  0.67 us (2%)
    all_to_all x1, waiting for transfers between devices, per_device(): lax.all_to_all(blocks, 'sec', split_axis=0, concat_axis=0, tiled=True)  22.9 us
    all_to_all x1, starting transfers between devices, per_device(): lax.all_to_all(blocks, 'sec', split_axis=0, concat_axis=0, tiled=True)  8.31 us
    ppermute x3, starting transfers between devices, per_device(): lax.ppermute(partial_sums, 'sec', [(i, i ^ other) for i in range(section_...  3.52 us
    ppermute x3, waiting for transfers between devices, per_device(): lax.ppermute(partial_sums, 'sec', [(i, i ^ other) for i in range(section_...  2.25 us
    pallas_call x1, Pallas kernels, per_device(): pl.pallas_call(resample_kernel, out_shape=jax.ShapeDtypeStruct(pencils.sh...  1.73 us
    pallas_call x1, Pallas kernels, per_device(): pl.pallas_call(sums_kernel, out_shape=jax.ShapeDtypeStruct((height, LANES...  0.88 us
    pallas_call x1, Pallas kernels, per_device(): pl.pallas_call(tables_kernel, out_shape=[jax.ShapeDtypeStruct((2 * LANES,...  0.86 us
  transfers between devices with their start and end apart: 4, of which 4 were waited for; matrix products, arithmetic and copies ran while one was open for 0% of the time, Pallas kernels for 2%

profile of v4, /device:TPU:0, one launch (start us, length us, event | category | flops | bytes accessed | tf_op | source)
XLA Modules:
  0.0 41.1 jit_solution(10515111651447379639)
XLA Ops:
  0.0 8.3 %all-to-all-start = ((bf16[16,16,2048]{2,1,0:T(8,128)(2,1)}), bf16[16,16,2048]{2,1,0:T(8,128)(2,1)S(1)}, u32[]{:S(2)}, u32[]{:S(2)}) async-start(bf16[16,16,2048]{2,1,0:T(8,128)(2,1)} %bitcast.2), calls=%async_computation | async-start | bytes 2097152 | tf_op jit(solution)/shard_map/all_to_all | solution.py:347
  8.3 0.0 copy-start.1
  8.3 0.0 copy-start
  8.4 0.0 copy-start.2
  8.4 0.6 %copy-done.1 = s32[4,32]{1,0:T(4,128)S(1)} copy-done((s32[4,32]{1,0:T(4,128)S(1)}, s32[4,32]{1,0:T(4,128)}, u32[]{:S(2)}) %copy-start.1) | copy-done | bytes 536
  9.0 0.0 copy-done
  9.0 0.0 copy-done.2
  9.0 0.9 %shard_map.46 = (bf16[256,128]{1,0:T(8,128)(2,1)S(1)}, bf16[128,2048]{1,0:T(8,128)(2,1)S(1)}, f32[16,128]{1,0:T(8,128)S(1)}, f32[17,128]{1,0:T(8,128)S(1)}) custom-call(s32[1]{0:T(128)} %bitcast.tile_row_ref, s32[17]{0:T(128)S(1)} %copy-done.2, s32[4,32]{1,0:T(4,128)S(1)} %copy-done, s32[4,32]{1,0:T(4,128)S(1)} %copy-done.1), custom_call_target="tpu_custom_call" | custom-call | flops 1048576 | bytes 1048576 | tf_op jit(solution)/shard_map/pallas_call | solution.py:353
  9.9 22.9 %all-to-all-done.x_ref.refs_4_ = bf16[16,16,2048]{2,1,0:T(8,128)(2,1)S(1)} async-done(((bf16[16,16,2048]{2,1,0:T(8,128)(2,1)}), bf16[16,16,2048]{2,1,0:T(8,128)(2,1)S(1)}, u32[]{:S(2)}, u32[]{:S(2)}) %all-to-all-start) | async-done | bytes 1048608 | tf_op jit(solution)/shard_map/all_to_all | solution.py:347
  32.8 0.9 %shard_map.47.refs_0_ = f32[24,128]{1,0:T(8,128)S(1)} custom-call(bf16[16,16,2048]{2,1,0:T(8,128)(2,1)S(1)} %all-to-all-done.x_ref.refs_4_, bf16[256,128]{1,0:T(8,128)(2,1)S(1)} %get-tuple-element.12.pairing_ref), custom_call_target="tpu_custom_call" | custom-call | flops 4194304 | bytes 1048576 | tf_op jit(solution)/shard_map/pallas_call | solution.py:368
  33.6 2.0 %collective-permute-start.2 = (f32[24,128]{1,0:T(8,128)S(1)}, f32[24,128]{1,0:T(8,128)S(1)}, u32[]{:S(2)}, u32[]{:S(2)}) collective-permute-start(f32[24,128]{1,0:T(8,128)S(1)} %shard_map.47.refs_0_), channel_id=1, source_target_pairs={{0,6},{2,4},{4,2},{6,0},{8,14},{10,12},{12,10},{14,8},{16,22},{18,... | collective-permute-start | bytes 36872 | tf_op jit(solution)/shard_map/ppermute | solution.py:390
  35.6 0.1 collective-permute-start.1
  35.7 1.4 %collective-permute-start = (f32[24,128]{1,0:T(8,128)S(1)}, f32[24,128]{1,0:T(8,128)S(1)}, u32[]{:S(2)}, u32[]{:S(2)}) collective-permute-start(f32[24,128]{1,0:T(8,128)S(1)} %shard_map.47.refs_0_), channel_id=1, source_target_pairs={{0,2},{2,0},{4,6},{6,4},{8,10},{10,8},{12,14},{14,12},{16,18},{18,... | collective-permute-start | bytes 36872 | tf_op jit(solution)/shard_map/ppermute | solution.py:390
  37.2 1.1 %collective-permute-done.2.refs_3_ = f32[24,128]{1,0:T(8,128)S(1)} collective-permute-done((f32[24,128]{1,0:T(8,128)S(1)}, f32[24,128]{1,0:T(8,128)S(1)}, u32[]{:S(2)}, u32[]{:S(2)}) %collective-permute-start.2) | collective-permute-done | bytes 12320 | tf_op jit(solution)/shard_map/ppermute | solution.py:390
  38.3 1.1 %collective-permute-done.1.refs_2_ = f32[24,128]{1,0:T(8,128)S(1)} collective-permute-done((f32[24,128]{1,0:T(8,128)S(1)}, f32[24,128]{1,0:T(8,128)S(1)}, u32[]{:S(2)}, u32[]{:S(2)}) %collective-permute-start.1) | collective-permute-done | bytes 12320 | tf_op jit(solution)/shard_map/ppermute | solution.py:390
  39.3 0.1 collective-permute-done.refs_1_
  39.4 1.7 %shard_map.48 = bf16[16,16,2048]{2,1,0:T(8,128)(2,1)} custom-call(f32[16,128]{1,0:T(8,128)S(1)} %get-tuple-element.9.fraction_ref, f32[17,128]{1,0:T(8,128)S(1)} %get-tuple-element.10.curve_ref, bf16[128,2048]{1,0:T(8,128)(2,1)S(1)} %get-tuple-element.11.to_pixels_ref, f32[24,128]{1,0:T(8,128)S(1)} %shard_map.47.refs_0_, ...), custom_call_target="tpu_custom_call" | custom-call | flops 16777216 | bytes 2097152 | tf_op jit(solution)/shard_map/pallas_call | solution.py:394
Async XLA Ops:
  0.0 32.8 %all-to-all-start = ((bf16[16,16,2048]{2,1,0:T(8,128)(2,1)}), bf16[16,16,2048]{2,1,0:T(8,128)(2,1)S(1)}, u32[]{:S(2)}, u32[]{:S(2)}) async-start(bf16[16,16,2048]{2,1,0:T(8,128)(2,1)} %bitcast.2), calls=%async_computation | async-start | bytes 2097152 | tf_op jit(solution)/shard_map/all_to_all | solution.py:347
  8.3 0.7 %copy-start.1 = (s32[4,32]{1,0:T(4,128)S(1)}, s32[4,32]{1,0:T(4,128)}, u32[]{:S(2)}) copy-start(s32[4,32]{1,0:T(4,128)} %step_ref.1) | copy-start | bytes 1540
  8.3 0.7 %copy-start = (s32[4,32]{1,0:T(4,128)S(1)}, s32[4,32]{1,0:T(4,128)}, u32[]{:S(2)}) copy-start(s32[4,32]{1,0:T(4,128)} %offset_ref.1) | copy-start | bytes 1540
  8.4 0.7 %copy-start.2 = (s32[17]{0:T(128)S(1)}, s32[17]{0:T(128)}, u32[]{:S(2)}) copy-start(s32[17]{0:T(128)} %knots_ref.1) | copy-start | bytes 208
  33.6 4.6 %collective-permute-start.2 = (f32[24,128]{1,0:T(8,128)S(1)}, f32[24,128]{1,0:T(8,128)S(1)}, u32[]{:S(2)}, u32[]{:S(2)}) collective-permute-start(f32[24,128]{1,0:T(8,128)S(1)} %shard_map.47.refs_0_), channel_id=1, source_target_pairs={{0,6},{2,4},{4,2},{6,0},{8,14},{10,12},{12,10},{14,8},{16,22},{18,... | collective-permute-start | bytes 36872 | tf_op jit(solution)/shard_map/ppermute | solution.py:390
  35.6 3.7 %collective-permute-start.1 = (f32[24,128]{1,0:T(8,128)S(1)}, f32[24,128]{1,0:T(8,128)S(1)}, u32[]{:S(2)}, u32[]{:S(2)}) collective-permute-start(f32[24,128]{1,0:T(8,128)S(1)} %shard_map.47.refs_0_), channel_id=1, source_target_pairs={{0,4},{2,6},{4,0},{6,2},{8,12},{10,14},{12,8},{14,10},{16,20},{18,... | collective-permute-start | bytes 36872 | tf_op jit(solution)/shard_map/ppermute | solution.py:390
  35.7 3.7 %collective-permute-start = (f32[24,128]{1,0:T(8,128)S(1)}, f32[24,128]{1,0:T(8,128)S(1)}, u32[]{:S(2)}, u32[]{:S(2)}) collective-permute-start(f32[24,128]{1,0:T(8,128)S(1)} %shard_map.47.refs_0_), channel_id=1, source_target_pairs={{0,2},{2,0},{4,6},{6,4},{8,10},{10,8},{12,14},{14,12},{16,18},{18,... | collective-permute-start | bytes 36872 | tf_op jit(solution)/shard_map/ppermute | solution.py:390

commit v5 on v4

--- a/solution.py
+++ b/solution.py
@@ -240,6 +240,13 @@
         sums_ref[8 * v : 8 * v + 8] = fold(pair[:8], pair[8:], 1, lanes[:8])
 
 
+def tree_sum(values):
+    while len(values) > 1:
+        rest = values[len(values) // 2 * 2 :]
+        values = [x + y for x, y in zip(values[::2], values[1::2])] + rest
+    return values[0]
+
+
 def resample_kernel(fraction_ref, curve_ref, to_pixels_ref, *refs):
     *sums_refs, x_ref, out_ref, spread_ref, made_ref, out_sems = refs
     sections, rows, cols = x_ref.shape
@@ -267,11 +274,14 @@
     for k in range(1, AHEAD + 1):
         covariance = quantity[k + 1] / samples - mean * shift_up(mean, k)
         correlation = covariance / jnp.sqrt(variance * shift_up(variance, k) + EPSILON)
-        distance = jnp.zeros((sections, tiles), jnp.float32)
         scaled = correlation * ((knots - 1) / 2.0)
-        for j in range(knots):
-            hat = jnp.maximum(0.0, 1.0 - jnp.abs(scaled - (j - (knots - 1) / 2.0)))
-            distance = distance + hat * curve_ref[j : j + 1, :]
+        distance = tree_sum(
+            [
+                jnp.maximum(0.0, 1.0 - jnp.abs(scaled - (j - (knots - 1) / 2.0)))
+                * curve_ref[j : j + 1, :]
+                for j in range(knots)
+            ]
+        )
         usable = (place + k < sections).astype(jnp.float32)
         numerator = numerator + usable * (k * distance)
         denominator = denominator + usable * float(k * k)
@@ -280,16 +290,13 @@
     for s in range(sections - 1):
         depths.append(depths[-1] + thickness[s : s + 1])
     target = depths[-1] * fraction_ref[...]
-    bracket = jnp.zeros((outputs, tiles), jnp.int32)
-    for s in range(1, sections):
-        bracket = bracket + (depths[s] <= target).astype(jnp.int32)
+    bracket = tree_sum(
+        [(depths[s] <= target).astype(jnp.int32) for s in range(1, sections)]
+    )
     bracket = jnp.minimum(bracket, sections - 2)
-    lower = jnp.zeros((outputs, tiles), jnp.float32)
-    upper = jnp.zeros((outputs, tiles), jnp.float32)
-    for s in range(sections - 1):
-        here = bracket == s
-        lower = jnp.where(here, depths[s], lower)
-        upper = jnp.where(here, depths[s + 1], upper)
+    here = [bracket == s for s in range(sections - 1)]
+    lower = tree_sum([jnp.where(h, depths[s], 0.0) for s, h in enumerate(here)])
+    upper = tree_sum([jnp.where(h, depths[s + 1], 0.0) for s, h in enumerate(here)])
     lifted = bracket.astype(jnp.float32) + (target - lower) / (upper - lower)
     beyond = lifted - bracket.astype(jnp.float32)
     pair = jnp.concatenate(

time: 41.4 us -> 41.4 us (level)
  no operation moved by 1% of the time
where the time goes in v5:
time: 41.4 us; the launch traced here: 41.2 us
  waiting for transfers between devices  25.1 us (61%)
  starting transfers between devices  11.8 us (29%)
  Pallas kernels  3.47 us (8%)
  local copies, waits for them, and re-layouts  0.67 us (2%)
    all_to_all x1, waiting for transfers between devices, per_device(): lax.all_to_all(blocks, 'sec', split_axis=0, concat_axis=0, tiled=True)  22.9 us
    all_to_all x1, starting transfers between devices, per_device(): lax.all_to_all(blocks, 'sec', split_axis=0, concat_axis=0, tiled=True)  8.31 us
    ppermute x3, starting transfers between devices, per_device(): lax.ppermute(partial_sums, 'sec', [(i, i ^ other) for i in range(section_...  3.52 us
    ppermute x3, waiting for transfers between devices, per_device(): lax.ppermute(partial_sums, 'sec', [(i, i ^ other) for i in range(section_...  2.25 us
    pallas_call x1, Pallas kernels, per_device(): pl.pallas_call(resample_kernel, out_shape=jax.ShapeDtypeStruct(pencils.sh...  1.73 us
    pallas_call x1, Pallas kernels, per_device(): pl.pallas_call(sums_kernel, out_shape=jax.ShapeDtypeStruct((height, LANES...  0.88 us
    pallas_call x1, Pallas kernels, per_device(): pl.pallas_call(tables_kernel, out_shape=[jax.ShapeDtypeStruct((2 * LANES,...  0.86 us
  transfers between devices with their start and end apart: 4, of which 4 were waited for; matrix products, arithmetic and copies ran while one was open for 0% of the time, Pallas kernels for 2%

profile of v5, /device:TPU:0, one launch (start us, length us, event | category | flops | bytes accessed | tf_op | source)
XLA Modules:
  0.0 41.2 jit_solution(13102114515273762698)
XLA Ops:
  0.0 8.3 %all-to-all-start = ((bf16[16,16,2048]{2,1,0:T(8,128)(2,1)}), bf16[16,16,2048]{2,1,0:T(8,128)(2,1)S(1)}, u32[]{:S(2)}, u32[]{:S(2)}) async-start(bf16[16,16,2048]{2,1,0:T(8,128)(2,1)} %bitcast.2), calls=%async_computation | async-start | bytes 2097152 | tf_op jit(solution)/shard_map/all_to_all | solution.py:354
  8.3 0.0 copy-start.1
  8.3 0.0 copy-start
  8.4 0.0 copy-start.2
  8.4 0.6 %copy-done.1 = s32[4,32]{1,0:T(4,128)S(1)} copy-done((s32[4,32]{1,0:T(4,128)S(1)}, s32[4,32]{1,0:T(4,128)}, u32[]{:S(2)}) %copy-start.1) | copy-done | bytes 536
  9.0 0.0 copy-done
  9.0 0.0 copy-done.2
  9.0 0.9 %shard_map.46 = (bf16[256,128]{1,0:T(8,128)(2,1)S(1)}, bf16[128,2048]{1,0:T(8,128)(2,1)S(1)}, f32[16,128]{1,0:T(8,128)S(1)}, f32[17,128]{1,0:T(8,128)S(1)}) custom-call(s32[1]{0:T(128)} %bitcast.tile_row_ref, s32[17]{0:T(128)S(1)} %copy-done.2, s32[4,32]{1,0:T(4,128)S(1)} %copy-done, s32[4,32]{1,0:T(4,128)S(1)} %copy-done.1), custom_call_target="tpu_custom_call" | custom-call | flops 1048576 | bytes 1048576 | tf_op jit(solution)/shard_map/pallas_call | solution.py:360
  9.9 22.9 %all-to-all-done.x_ref.refs_4_ = bf16[16,16,2048]{2,1,0:T(8,128)(2,1)S(1)} async-done(((bf16[16,16,2048]{2,1,0:T(8,128)(2,1)}), bf16[16,16,2048]{2,1,0:T(8,128)(2,1)S(1)}, u32[]{:S(2)}, u32[]{:S(2)}) %all-to-all-start) | async-done | bytes 1048608 | tf_op jit(solution)/shard_map/all_to_all | solution.py:354
  32.8 0.9 %shard_map.47.refs_0_ = f32[24,128]{1,0:T(8,128)S(1)} custom-call(bf16[16,16,2048]{2,1,0:T(8,128)(2,1)S(1)} %all-to-all-done.x_ref.refs_4_, bf16[256,128]{1,0:T(8,128)(2,1)S(1)} %get-tuple-element.12.pairing_ref), custom_call_target="tpu_custom_call" | custom-call | flops 4194304 | bytes 1048576 | tf_op jit(solution)/shard_map/pallas_call | solution.py:375
  33.6 2.0 %collective-permute-start.2 = (f32[24,128]{1,0:T(8,128)S(1)}, f32[24,128]{1,0:T(8,128)S(1)}, u32[]{:S(2)}, u32[]{:S(2)}) collective-permute-start(f32[24,128]{1,0:T(8,128)S(1)} %shard_map.47.refs_0_), channel_id=1, source_target_pairs={{0,6},{2,4},{4,2},{6,0},{8,14},{10,12},{12,10},{14,8},{16,22},{18,... | collective-permute-start | bytes 36872 | tf_op jit(solution)/shard_map/ppermute | solution.py:397
  35.6 0.1 collective-permute-start.1
  35.7 1.4 %collective-permute-start = (f32[24,128]{1,0:T(8,128)S(1)}, f32[24,128]{1,0:T(8,128)S(1)}, u32[]{:S(2)}, u32[]{:S(2)}) collective-permute-start(f32[24,128]{1,0:T(8,128)S(1)} %shard_map.47.refs_0_), channel_id=1, source_target_pairs={{0,2},{2,0},{4,6},{6,4},{8,10},{10,8},{12,14},{14,12},{16,18},{18,... | collective-permute-start | bytes 36872 | tf_op jit(solution)/shard_map/ppermute | solution.py:397
  37.2 1.1 %collective-permute-done.2.refs_3_ = f32[24,128]{1,0:T(8,128)S(1)} collective-permute-done((f32[24,128]{1,0:T(8,128)S(1)}, f32[24,128]{1,0:T(8,128)S(1)}, u32[]{:S(2)}, u32[]{:S(2)}) %collective-permute-start.2) | collective-permute-done | bytes 12320 | tf_op jit(solution)/shard_map/ppermute | solution.py:397
  38.3 1.1 %collective-permute-done.1.refs_2_ = f32[24,128]{1,0:T(8,128)S(1)} collective-permute-done((f32[24,128]{1,0:T(8,128)S(1)}, f32[24,128]{1,0:T(8,128)S(1)}, u32[]{:S(2)}, u32[]{:S(2)}) %collective-permute-start.1) | collective-permute-done | bytes 12320 | tf_op jit(solution)/shard_map/ppermute | solution.py:397
  39.3 0.1 collective-permute-done.refs_1_
  39.4 1.7 %shard_map.48 = bf16[16,16,2048]{2,1,0:T(8,128)(2,1)} custom-call(f32[16,128]{1,0:T(8,128)S(1)} %get-tuple-element.9.fraction_ref, f32[17,128]{1,0:T(8,128)S(1)} %get-tuple-element.10.curve_ref, bf16[128,2048]{1,0:T(8,128)(2,1)S(1)} %get-tuple-element.11.to_pixels_ref, f32[24,128]{1,0:T(8,128)S(1)} %shard_map.47.refs_0_, ...), custom_call_target="tpu_custom_call" | custom-call | flops 16777216 | bytes 2097152 | tf_op jit(solution)/shard_map/pallas_call | solution.py:401
Async XLA Ops:
  0.0 32.8 %all-to-all-start = ((bf16[16,16,2048]{2,1,0:T(8,128)(2,1)}), bf16[16,16,2048]{2,1,0:T(8,128)(2,1)S(1)}, u32[]{:S(2)}, u32[]{:S(2)}) async-start(bf16[16,16,2048]{2,1,0:T(8,128)(2,1)} %bitcast.2), calls=%async_computation | async-start | bytes 2097152 | tf_op jit(solution)/shard_map/all_to_all | solution.py:354
  8.3 0.7 %copy-start.1 = (s32[4,32]{1,0:T(4,128)S(1)}, s32[4,32]{1,0:T(4,128)}, u32[]{:S(2)}) copy-start(s32[4,32]{1,0:T(4,128)} %step_ref.1) | copy-start | bytes 1540
  8.3 0.7 %copy-start = (s32[4,32]{1,0:T(4,128)S(1)}, s32[4,32]{1,0:T(4,128)}, u32[]{:S(2)}) copy-start(s32[4,32]{1,0:T(4,128)} %offset_ref.1) | copy-start | bytes 1540
  8.4 0.7 %copy-start.2 = (s32[17]{0:T(128)S(1)}, s32[17]{0:T(128)}, u32[]{:S(2)}) copy-start(s32[17]{0:T(128)} %knots_ref.1) | copy-start | bytes 208
  33.6 4.6 %collective-permute-start.2 = (f32[24,128]{1,0:T(8,128)S(1)}, f32[24,128]{1,0:T(8,128)S(1)}, u32[]{:S(2)}, u32[]{:S(2)}) collective-permute-start(f32[24,128]{1,0:T(8,128)S(1)} %shard_map.47.refs_0_), channel_id=1, source_target_pairs={{0,6},{2,4},{4,2},{6,0},{8,14},{10,12},{12,10},{14,8},{16,22},{18,... | collective-permute-start | bytes 36872 | tf_op jit(solution)/shard_map/ppermute | solution.py:397
  35.6 3.7 %collective-permute-start.1 = (f32[24,128]{1,0:T(8,128)S(1)}, f32[24,128]{1,0:T(8,128)S(1)}, u32[]{:S(2)}, u32[]{:S(2)}) collective-permute-start(f32[24,128]{1,0:T(8,128)S(1)} %shard_map.47.refs_0_), channel_id=1, source_target_pairs={{0,4},{2,6},{4,0},{6,2},{8,12},{10,14},{12,8},{14,10},{16,20},{18,... | collective-permute-start | bytes 36872 | tf_op jit(solution)/shard_map/ppermute | solution.py:397
  35.7 3.7 %collective-permute-start = (f32[24,128]{1,0:T(8,128)S(1)}, f32[24,128]{1,0:T(8,128)S(1)}, u32[]{:S(2)}, u32[]{:S(2)}) collective-permute-start(f32[24,128]{1,0:T(8,128)S(1)} %shard_map.47.refs_0_), channel_id=1, source_target_pairs={{0,2},{2,0},{4,6},{6,4},{8,10},{10,8},{12,14},{14,12},{16,18},{18,... | collective-permute-start | bytes 36872 | tf_op jit(solution)/shard_map/ppermute | solution.py:397

commit v6 on v5

--- a/solution.py
+++ b/solution.py
@@ -164,7 +164,7 @@
     fraction_ref,
     curve_ref,
 ):
-    pairing_ref[...] = one_hot(pairing_ref.shape, lambda r: r // 2, lambda c: c)
+    pairing_ref[...] = 0.25 * one_hot(pairing_ref.shape, lambda r: r // 2, lambda c: c)
     to_pixels_ref[...] = one_hot(
         to_pixels_ref.shape,
         lambda r: jnp.where(r % 4 == 0, tile_of_lane(r), -1),
@@ -222,7 +222,7 @@
         for r in range(rows // 2):
             upper = pairs_ref[g, pl.ds(2 * r, sections, stride=17), :]
             lower = pairs_ref[g, pl.ds(2 * r + 1, sections, stride=17), :]
-            reduced = ((upper + lower) * 0.25).astype(jnp.bfloat16).astype(jnp.float32)
+            reduced = (upper + lower).astype(jnp.bfloat16).astype(jnp.float32)
             reduced_ref[g, r, :sections] = reduced
             reduced_ref[g, r, sections:] = jnp.zeros((8, LANES), jnp.float32)
             total[0] = total[0] + reduced

time: 41.4 us -> 41.3 us (level)
  no operation moved by 1% of the time
where the time goes in v6:
time: 41.3 us; the launch traced here: 41.1 us
  waiting for transfers between devices  25.1 us (61%)
  starting transfers between devices  11.8 us (29%)
  Pallas kernels  3.46 us (8%)
  local copies, waits for them, and re-layouts  0.67 us (2%)
    all_to_all x1, waiting for transfers between devices, per_device(): lax.all_to_all(blocks, 'sec', split_axis=0, concat_axis=0, tiled=True)  22.9 us
    all_to_all x1, starting transfers between devices, per_device(): lax.all_to_all(blocks, 'sec', split_axis=0, concat_axis=0, tiled=True)  8.31 us
    ppermute x3, starting transfers between devices, per_device(): lax.ppermute(partial_sums, 'sec', [(i, i ^ other) for i in range(section_...  3.52 us
    ppermute x3, waiting for transfers between devices, per_device(): lax.ppermute(partial_sums, 'sec', [(i, i ^ other) for i in range(section_...  2.25 us
    pallas_call x1, Pallas kernels, per_device(): pl.pallas_call(resample_kernel, out_shape=jax.ShapeDtypeStruct(pencils.sh...  1.73 us
    pallas_call x1, Pallas kernels, per_device(): pl.pallas_call(tables_kernel, out_shape=[jax.ShapeDtypeStruct((2 * LANES,...  0.87 us
    pallas_call x1, Pallas kernels, per_device(): pl.pallas_call(sums_kernel, out_shape=jax.ShapeDtypeStruct((height, LANES...  0.86 us
  transfers between devices with their start and end apart: 4, of which 4 were waited for; matrix products, arithmetic and copies ran while one was open for 0% of the time, Pallas kernels for 2%

profile of v6, /device:TPU:0, one launch (start us, length us, event | category | flops | bytes accessed | tf_op | source)
XLA Modules:
  0.0 41.1 jit_solution(13042434735243828998)
XLA Ops:
  0.0 8.3 %all-to-all-start = ((bf16[16,16,2048]{2,1,0:T(8,128)(2,1)}), bf16[16,16,2048]{2,1,0:T(8,128)(2,1)S(1)}, u32[]{:S(2)}, u32[]{:S(2)}) async-start(bf16[16,16,2048]{2,1,0:T(8,128)(2,1)} %bitcast.2), calls=%async_computation | async-start | bytes 2097152 | tf_op jit(solution)/shard_map/all_to_all | solution.py:354
  8.3 0.0 copy-start.1
  8.3 0.0 copy-start
  8.4 0.0 copy-start.2
  8.4 0.6 %copy-done.1 = s32[4,32]{1,0:T(4,128)S(1)} copy-done((s32[4,32]{1,0:T(4,128)S(1)}, s32[4,32]{1,0:T(4,128)}, u32[]{:S(2)}) %copy-start.1) | copy-done | bytes 536
  9.0 0.0 copy-done
  9.0 0.0 copy-done.2
  9.0 0.9 %shard_map.46 = (bf16[256,128]{1,0:T(8,128)(2,1)S(1)}, bf16[128,2048]{1,0:T(8,128)(2,1)S(1)}, f32[16,128]{1,0:T(8,128)S(1)}, f32[17,128]{1,0:T(8,128)S(1)}) custom-call(s32[1]{0:T(128)} %bitcast.tile_row_ref, s32[17]{0:T(128)S(1)} %copy-done.2, s32[4,32]{1,0:T(4,128)S(1)} %copy-done, s32[4,32]{1,0:T(4,128)S(1)} %copy-done.1), custom_call_target="tpu_custom_call" | custom-call | flops 1048576 | bytes 1048576 | tf_op jit(solution)/shard_map/pallas_call | solution.py:360
  9.9 22.9 %all-to-all-done.x_ref.refs_4_ = bf16[16,16,2048]{2,1,0:T(8,128)(2,1)S(1)} async-done(((bf16[16,16,2048]{2,1,0:T(8,128)(2,1)}), bf16[16,16,2048]{2,1,0:T(8,128)(2,1)S(1)}, u32[]{:S(2)}, u32[]{:S(2)}) %all-to-all-start) | async-done | bytes 1048608 | tf_op jit(solution)/shard_map/all_to_all | solution.py:354
  32.8 0.9 %shard_map.47.refs_0_ = f32[24,128]{1,0:T(8,128)S(1)} custom-call(bf16[16,16,2048]{2,1,0:T(8,128)(2,1)S(1)} %all-to-all-done.x_ref.refs_4_, bf16[256,128]{1,0:T(8,128)(2,1)S(1)} %get-tuple-element.12.pairing_ref), custom_call_target="tpu_custom_call" | custom-call | flops 4194304 | bytes 1048576 | tf_op jit(solution)/shard_map/pallas_call | solution.py:375
  33.6 2.0 %collective-permute-start.2 = (f32[24,128]{1,0:T(8,128)S(1)}, f32[24,128]{1,0:T(8,128)S(1)}, u32[]{:S(2)}, u32[]{:S(2)}) collective-permute-start(f32[24,128]{1,0:T(8,128)S(1)} %shard_map.47.refs_0_), channel_id=1, source_target_pairs={{0,6},{2,4},{4,2},{6,0},{8,14},{10,12},{12,10},{14,8},{16,22},{18,... | collective-permute-start | bytes 36872 | tf_op jit(solution)/shard_map/ppermute | solution.py:397
  35.6 0.1 collective-permute-start.1
  35.7 1.4 %collective-permute-start = (f32[24,128]{1,0:T(8,128)S(1)}, f32[24,128]{1,0:T(8,128)S(1)}, u32[]{:S(2)}, u32[]{:S(2)}) collective-permute-start(f32[24,128]{1,0:T(8,128)S(1)} %shard_map.47.refs_0_), channel_id=1, source_target_pairs={{0,2},{2,0},{4,6},{6,4},{8,10},{10,8},{12,14},{14,12},{16,18},{18,... | collective-permute-start | bytes 36872 | tf_op jit(solution)/shard_map/ppermute | solution.py:397
  37.2 1.1 %collective-permute-done.2.refs_3_ = f32[24,128]{1,0:T(8,128)S(1)} collective-permute-done((f32[24,128]{1,0:T(8,128)S(1)}, f32[24,128]{1,0:T(8,128)S(1)}, u32[]{:S(2)}, u32[]{:S(2)}) %collective-permute-start.2) | collective-permute-done | bytes 12320 | tf_op jit(solution)/shard_map/ppermute | solution.py:397
  38.3 1.1 %collective-permute-done.1.refs_2_ = f32[24,128]{1,0:T(8,128)S(1)} collective-permute-done((f32[24,128]{1,0:T(8,128)S(1)}, f32[24,128]{1,0:T(8,128)S(1)}, u32[]{:S(2)}, u32[]{:S(2)}) %collective-permute-start.1) | collective-permute-done | bytes 12320 | tf_op jit(solution)/shard_map/ppermute | solution.py:397
  39.3 0.1 collective-permute-done.refs_1_
  39.4 1.7 %shard_map.48 = bf16[16,16,2048]{2,1,0:T(8,128)(2,1)} custom-call(f32[16,128]{1,0:T(8,128)S(1)} %get-tuple-element.9.fraction_ref, f32[17,128]{1,0:T(8,128)S(1)} %get-tuple-element.10.curve_ref, bf16[128,2048]{1,0:T(8,128)(2,1)S(1)} %get-tuple-element.11.to_pixels_ref, f32[24,128]{1,0:T(8,128)S(1)} %shard_map.47.refs_0_, ...), custom_call_target="tpu_custom_call" | custom-call | flops 16777216 | bytes 2097152 | tf_op jit(solution)/shard_map/pallas_call | solution.py:401
Async XLA Ops:
  0.0 32.8 %all-to-all-start = ((bf16[16,16,2048]{2,1,0:T(8,128)(2,1)}), bf16[16,16,2048]{2,1,0:T(8,128)(2,1)S(1)}, u32[]{:S(2)}, u32[]{:S(2)}) async-start(bf16[16,16,2048]{2,1,0:T(8,128)(2,1)} %bitcast.2), calls=%async_computation | async-start | bytes 2097152 | tf_op jit(solution)/shard_map/all_to_all | solution.py:354
  8.3 0.7 %copy-start.1 = (s32[4,32]{1,0:T(4,128)S(1)}, s32[4,32]{1,0:T(4,128)}, u32[]{:S(2)}) copy-start(s32[4,32]{1,0:T(4,128)} %step_ref.1) | copy-start | bytes 1540
  8.3 0.7 %copy-start = (s32[4,32]{1,0:T(4,128)S(1)}, s32[4,32]{1,0:T(4,128)}, u32[]{:S(2)}) copy-start(s32[4,32]{1,0:T(4,128)} %offset_ref.1) | copy-start | bytes 1540
  8.4 0.7 %copy-start.2 = (s32[17]{0:T(128)S(1)}, s32[17]{0:T(128)}, u32[]{:S(2)}) copy-start(s32[17]{0:T(128)} %knots_ref.1) | copy-start | bytes 208
  33.6 4.6 %collective-permute-start.2 = (f32[24,128]{1,0:T(8,128)S(1)}, f32[24,128]{1,0:T(8,128)S(1)}, u32[]{:S(2)}, u32[]{:S(2)}) collective-permute-start(f32[24,128]{1,0:T(8,128)S(1)} %shard_map.47.refs_0_), channel_id=1, source_target_pairs={{0,6},{2,4},{4,2},{6,0},{8,14},{10,12},{12,10},{14,8},{16,22},{18,... | collective-permute-start | bytes 36872 | tf_op jit(solution)/shard_map/ppermute | solution.py:397
  35.6 3.7 %collective-permute-start.1 = (f32[24,128]{1,0:T(8,128)S(1)}, f32[24,128]{1,0:T(8,128)S(1)}, u32[]{:S(2)}, u32[]{:S(2)}) collective-permute-start(f32[24,128]{1,0:T(8,128)S(1)} %shard_map.47.refs_0_), channel_id=1, source_target_pairs={{0,4},{2,6},{4,0},{6,2},{8,12},{10,14},{12,8},{14,10},{16,20},{18,... | collective-permute-start | bytes 36872 | tf_op jit(solution)/shard_map/ppermute | solution.py:397
  35.7 3.7 %collective-permute-start = (f32[24,128]{1,0:T(8,128)S(1)}, f32[24,128]{1,0:T(8,128)S(1)}, u32[]{:S(2)}, u32[]{:S(2)}) collective-permute-start(f32[24,128]{1,0:T(8,128)S(1)} %shard_map.47.refs_0_), channel_id=1, source_target_pairs={{0,2},{2,0},{4,6},{6,4},{8,10},{10,8},{12,14},{14,12},{16,18},{18,... | collective-permute-start | bytes 36872 | tf_op jit(solution)/shard_map/ppermute | solution.py:397

commit v7 on v6

--- a/solution.py
+++ b/solution.py
@@ -252,7 +252,7 @@
     sections, rows, cols = x_ref.shape
     outputs = out_ref.shape[0]
     tiles = LANES
-    samples = float((TILE // 2) ** 2)
+    share = 1.0 / float((TILE // 2) ** 2)
     packed = sums_refs[0][...]
     for ref in sums_refs[1:]:
         packed = packed + ref[...]
@@ -265,14 +265,14 @@
     quantity = [
         jnp.concatenate([unpack(q, 0), unpack(q, 1)], axis=0) for q in range(AHEAD + 2)
     ]
-    mean = quantity[0] / samples
-    variance = quantity[1] / samples - mean * mean
+    mean = quantity[0] * share
+    variance = quantity[1] * share - mean * mean
     place = lax.broadcasted_iota(jnp.int32, (sections, tiles), 0)
     numerator = jnp.zeros((sections, tiles), jnp.float32)
     denominator = jnp.zeros((sections, tiles), jnp.float32)
     knots = curve_ref.shape[0]
     for k in range(1, AHEAD + 1):
-        covariance = quantity[k + 1] / samples - mean * shift_up(mean, k)
+        covariance = quantity[k + 1] * share - mean * shift_up(mean, k)
         correlation = covariance / jnp.sqrt(variance * shift_up(variance, k) + EPSILON)
         scaled = correlation * ((knots - 1) / 2.0)
         distance = tree_sum(

time: 41.3 us -> 41.3 us (level)
  no operation moved by 1% of the time
where the time goes in v7:
time: 41.3 us; the launch traced here: 41.1 us
  waiting for transfers between devices  25.1 us (61%)
  starting transfers between devices  11.8 us (29%)
  Pallas kernels  3.46 us (8%)
  local copies, waits for them, and re-layouts  0.67 us (2%)
    all_to_all x1, waiting for transfers between devices, per_device(): lax.all_to_all(blocks, 'sec', split_axis=0, concat_axis=0, tiled=True)  22.9 us
    all_to_all x1, starting transfers between devices, per_device(): lax.all_to_all(blocks, 'sec', split_axis=0, concat_axis=0, tiled=True)  8.31 us
    ppermute x3, starting transfers between devices, per_device(): lax.ppermute(partial_sums, 'sec', [(i, i ^ other) for i in range(section_...  3.52 us
    ppermute x3, waiting for transfers between devices, per_device(): lax.ppermute(partial_sums, 'sec', [(i, i ^ other) for i in range(section_...  2.25 us
    pallas_call x1, Pallas kernels, per_device(): pl.pallas_call(resample_kernel, out_shape=jax.ShapeDtypeStruct(pencils.sh...  1.73 us
    pallas_call x1, Pallas kernels, per_device(): pl.pallas_call(tables_kernel, out_shape=[jax.ShapeDtypeStruct((2 * LANES,...  0.87 us
    pallas_call x1, Pallas kernels, per_device(): pl.pallas_call(sums_kernel, out_shape=jax.ShapeDtypeStruct((height, LANES...  0.86 us
  transfers between devices with their start and end apart: 4, of which 4 were waited for; matrix products, arithmetic and copies ran while one was open for 0% of the time, Pallas kernels for 2%

profile of v7, /device:TPU:0, one launch (start us, length us, event | category | flops | bytes accessed | tf_op | source)
XLA Modules:
  0.0 41.1 jit_solution(13042434735243828998)
XLA Ops:
  0.0 8.3 %all-to-all-start = ((bf16[16,16,2048]{2,1,0:T(8,128)(2,1)}), bf16[16,16,2048]{2,1,0:T(8,128)(2,1)S(1)}, u32[]{:S(2)}, u32[]{:S(2)}) async-start(bf16[16,16,2048]{2,1,0:T(8,128)(2,1)} %bitcast.2), calls=%async_computation | async-start | bytes 2097152 | tf_op jit(solution)/shard_map/all_to_all | solution.py:354
  8.3 0.0 copy-start.1
  8.3 0.0 copy-start
  8.4 0.0 copy-start.2
  8.4 0.6 %copy-done.1 = s32[4,32]{1,0:T(4,128)S(1)} copy-done((s32[4,32]{1,0:T(4,128)S(1)}, s32[4,32]{1,0:T(4,128)}, u32[]{:S(2)}) %copy-start.1) | copy-done | bytes 536
  9.0 0.0 copy-done
  9.0 0.0 copy-done.2
  9.0 0.9 %shard_map.46 = (bf16[256,128]{1,0:T(8,128)(2,1)S(1)}, bf16[128,2048]{1,0:T(8,128)(2,1)S(1)}, f32[16,128]{1,0:T(8,128)S(1)}, f32[17,128]{1,0:T(8,128)S(1)}) custom-call(s32[1]{0:T(128)} %bitcast.tile_row_ref, s32[17]{0:T(128)S(1)} %copy-done.2, s32[4,32]{1,0:T(4,128)S(1)} %copy-done, s32[4,32]{1,0:T(4,128)S(1)} %copy-done.1), custom_call_target="tpu_custom_call" | custom-call | flops 1048576 | bytes 1048576 | tf_op jit(solution)/shard_map/pallas_call | solution.py:360
  9.9 22.9 %all-to-all-done.x_ref.refs_4_ = bf16[16,16,2048]{2,1,0:T(8,128)(2,1)S(1)} async-done(((bf16[16,16,2048]{2,1,0:T(8,128)(2,1)}), bf16[16,16,2048]{2,1,0:T(8,128)(2,1)S(1)}, u32[]{:S(2)}, u32[]{:S(2)}) %all-to-all-start) | async-done | bytes 1048608 | tf_op jit(solution)/shard_map/all_to_all | solution.py:354
  32.8 0.9 %shard_map.47.refs_0_ = f32[24,128]{1,0:T(8,128)S(1)} custom-call(bf16[16,16,2048]{2,1,0:T(8,128)(2,1)S(1)} %all-to-all-done.x_ref.refs_4_, bf16[256,128]{1,0:T(8,128)(2,1)S(1)} %get-tuple-element.12.pairing_ref), custom_call_target="tpu_custom_call" | custom-call | flops 4194304 | bytes 1048576 | tf_op jit(solution)/shard_map/pallas_call | solution.py:375
  33.6 2.0 %collective-permute-start.2 = (f32[24,128]{1,0:T(8,128)S(1)}, f32[24,128]{1,0:T(8,128)S(1)}, u32[]{:S(2)}, u32[]{:S(2)}) collective-permute-start(f32[24,128]{1,0:T(8,128)S(1)} %shard_map.47.refs_0_), channel_id=1, source_target_pairs={{0,6},{2,4},{4,2},{6,0},{8,14},{10,12},{12,10},{14,8},{16,22},{18,... | collective-permute-start | bytes 36872 | tf_op jit(solution)/shard_map/ppermute | solution.py:397
  35.6 0.1 collective-permute-start.1
  35.7 1.4 %collective-permute-start = (f32[24,128]{1,0:T(8,128)S(1)}, f32[24,128]{1,0:T(8,128)S(1)}, u32[]{:S(2)}, u32[]{:S(2)}) collective-permute-start(f32[24,128]{1,0:T(8,128)S(1)} %shard_map.47.refs_0_), channel_id=1, source_target_pairs={{0,2},{2,0},{4,6},{6,4},{8,10},{10,8},{12,14},{14,12},{16,18},{18,... | collective-permute-start | bytes 36872 | tf_op jit(solution)/shard_map/ppermute | solution.py:397
  37.2 1.1 %collective-permute-done.2.refs_3_ = f32[24,128]{1,0:T(8,128)S(1)} collective-permute-done((f32[24,128]{1,0:T(8,128)S(1)}, f32[24,128]{1,0:T(8,128)S(1)}, u32[]{:S(2)}, u32[]{:S(2)}) %collective-permute-start.2) | collective-permute-done | bytes 12320 | tf_op jit(solution)/shard_map/ppermute | solution.py:397
  38.3 1.1 %collective-permute-done.1.refs_2_ = f32[24,128]{1,0:T(8,128)S(1)} collective-permute-done((f32[24,128]{1,0:T(8,128)S(1)}, f32[24,128]{1,0:T(8,128)S(1)}, u32[]{:S(2)}, u32[]{:S(2)}) %collective-permute-start.1) | collective-permute-done | bytes 12320 | tf_op jit(solution)/shard_map/ppermute | solution.py:397
  39.3 0.1 collective-permute-done.refs_1_
  39.4 1.7 %shard_map.48 = bf16[16,16,2048]{2,1,0:T(8,128)(2,1)} custom-call(f32[16,128]{1,0:T(8,128)S(1)} %get-tuple-element.9.fraction_ref, f32[17,128]{1,0:T(8,128)S(1)} %get-tuple-element.10.curve_ref, bf16[128,2048]{1,0:T(8,128)(2,1)S(1)} %get-tuple-element.11.to_pixels_ref, f32[24,128]{1,0:T(8,128)S(1)} %shard_map.47.refs_0_, ...), custom_call_target="tpu_custom_call" | custom-call | flops 16777216 | bytes 2097152 | tf_op jit(solution)/shard_map/pallas_call | solution.py:401
Async XLA Ops:
  0.0 32.8 %all-to-all-start = ((bf16[16,16,2048]{2,1,0:T(8,128)(2,1)}), bf16[16,16,2048]{2,1,0:T(8,128)(2,1)S(1)}, u32[]{:S(2)}, u32[]{:S(2)}) async-start(bf16[16,16,2048]{2,1,0:T(8,128)(2,1)} %bitcast.2), calls=%async_computation | async-start | bytes 2097152 | tf_op jit(solution)/shard_map/all_to_all | solution.py:354
  8.3 0.7 %copy-start.1 = (s32[4,32]{1,0:T(4,128)S(1)}, s32[4,32]{1,0:T(4,128)}, u32[]{:S(2)}) copy-start(s32[4,32]{1,0:T(4,128)} %step_ref.1) | copy-start | bytes 1540
  8.3 0.7 %copy-start = (s32[4,32]{1,0:T(4,128)S(1)}, s32[4,32]{1,0:T(4,128)}, u32[]{:S(2)}) copy-start(s32[4,32]{1,0:T(4,128)} %offset_ref.1) | copy-start | bytes 1540
  8.4 0.7 %copy-start.2 = (s32[17]{0:T(128)S(1)}, s32[17]{0:T(128)}, u32[]{:S(2)}) copy-start(s32[17]{0:T(128)} %knots_ref.1) | copy-start | bytes 208
  33.6 4.6 %collective-permute-start.2 = (f32[24,128]{1,0:T(8,128)S(1)}, f32[24,128]{1,0:T(8,128)S(1)}, u32[]{:S(2)}, u32[]{:S(2)}) collective-permute-start(f32[24,128]{1,0:T(8,128)S(1)} %shard_map.47.refs_0_), channel_id=1, source_target_pairs={{0,6},{2,4},{4,2},{6,0},{8,14},{10,12},{12,10},{14,8},{16,22},{18,... | collective-permute-start | bytes 36872 | tf_op jit(solution)/shard_map/ppermute | solution.py:397
  35.6 3.7 %collective-permute-start.1 = (f32[24,128]{1,0:T(8,128)S(1)}, f32[24,128]{1,0:T(8,128)S(1)}, u32[]{:S(2)}, u32[]{:S(2)}) collective-permute-start(f32[24,128]{1,0:T(8,128)S(1)} %shard_map.47.refs_0_), channel_id=1, source_target_pairs={{0,4},{2,6},{4,0},{6,2},{8,12},{10,14},{12,8},{14,10},{16,20},{18,... | collective-permute-start | bytes 36872 | tf_op jit(solution)/shard_map/ppermute | solution.py:397
  35.7 3.7 %collective-permute-start = (f32[24,128]{1,0:T(8,128)S(1)}, f32[24,128]{1,0:T(8,128)S(1)}, u32[]{:S(2)}, u32[]{:S(2)}) collective-permute-start(f32[24,128]{1,0:T(8,128)S(1)} %shard_map.47.refs_0_), channel_id=1, source_target_pairs={{0,2},{2,0},{4,6},{6,4},{8,10},{10,8},{12,14},{14,12},{16,18},{18,... | collective-permute-start | bytes 36872 | tf_op jit(solution)/shard_map/ppermute | solution.py:397

commit v8 on v6

--- a/solution.py
+++ b/solution.py
@@ -217,6 +217,9 @@
             pairs_ref[g, pl.ds(17 * s, rows), :] = pairs[rows * s : rows * (s + 1)]
     lanes = lax.broadcasted_iota(jnp.int32, (sections, LANES), 1)
     waiting = {}
+    reduced_ref[:, :, sections:, :] = jnp.zeros(
+        reduced_ref.shape[:2] + (8, LANES), jnp.float32
+    )
     for g in range(groups):
         total = [jnp.zeros((sections, LANES), jnp.float32)] * (AHEAD + 2)
         for r in range(rows // 2):
@@ -224,7 +227,6 @@
             lower = pairs_ref[g, pl.ds(2 * r + 1, sections, stride=17), :]
             reduced = (upper + lower).astype(jnp.bfloat16).astype(jnp.float32)
             reduced_ref[g, r, :sections] = reduced
-            reduced_ref[g, r, sections:] = jnp.zeros((8, LANES), jnp.float32)
             total[0] = total[0] + reduced
             total[1] = total[1] + reduced * reduced
             for k in range(1, AHEAD + 1):

time: 41.3 us -> 41.3 us (level)
  no operation moved by 1% of the time
where the time goes in v8:
time: 41.3 us; the launch traced here: 41.1 us
  waiting for transfers between devices  25.1 us (61%)
  starting transfers between devices  11.8 us (29%)
  Pallas kernels  3.46 us (8%)
  local copies, waits for them, and re-layouts  0.67 us (2%)
    all_to_all x1, waiting for transfers between devices, per_device(): lax.all_to_all(blocks, 'sec', split_axis=0, concat_axis=0, tiled=True)  22.9 us
    all_to_all x1, starting transfers between devices, per_device(): lax.all_to_all(blocks, 'sec', split_axis=0, concat_axis=0, tiled=True)  8.31 us
    ppermute x3, starting transfers between devices, per_device(): lax.ppermute(partial_sums, 'sec', [(i, i ^ other) for i in range(section_...  3.52 us
    ppermute x3, waiting for transfers between devices, per_device(): lax.ppermute(partial_sums, 'sec', [(i, i ^ other) for i in range(section_...  2.25 us
    pallas_call x1, Pallas kernels, per_device(): pl.pallas_call(resample_kernel, out_shape=jax.ShapeDtypeStruct(pencils.sh...  1.73 us
    pallas_call x1, Pallas kernels, per_device(): pl.pallas_call(tables_kernel, out_shape=[jax.ShapeDtypeStruct((2 * LANES,...  0.87 us
    pallas_call x1, Pallas kernels, per_device(): pl.pallas_call(sums_kernel, out_shape=jax.ShapeDtypeStruct((height, LANES...  0.86 us
  transfers between devices with their start and end apart: 4, of which 4 were waited for; matrix products, arithmetic and copies ran while one was open for 0% of the time, Pallas kernels for 2%

profile of v8, /device:TPU:0, one launch (start us, length us, event | category | flops | bytes accessed | tf_op | source)
XLA Modules:
  0.0 41.1 jit_solution(13042434735243828998)
XLA Ops:
  0.0 8.3 %all-to-all-start = ((bf16[16,16,2048]{2,1,0:T(8,128)(2,1)}), bf16[16,16,2048]{2,1,0:T(8,128)(2,1)S(1)}, u32[]{:S(2)}, u32[]{:S(2)}) async-start(bf16[16,16,2048]{2,1,0:T(8,128)(2,1)} %bitcast.2), calls=%async_computation | async-start | bytes 2097152 | tf_op jit(solution)/shard_map/all_to_all | solution.py:356
  8.3 0.0 copy-start.1
  8.3 0.0 copy-start
  8.4 0.0 copy-start.2
  8.4 0.6 %copy-done.1 = s32[4,32]{1,0:T(4,128)S(1)} copy-done((s32[4,32]{1,0:T(4,128)S(1)}, s32[4,32]{1,0:T(4,128)}, u32[]{:S(2)}) %copy-start.1) | copy-done | bytes 536
  9.0 0.0 copy-done
  9.0 0.0 copy-done.2
  9.0 0.9 %shard_map.46 = (bf16[256,128]{1,0:T(8,128)(2,1)S(1)}, bf16[128,2048]{1,0:T(8,128)(2,1)S(1)}, f32[16,128]{1,0:T(8,128)S(1)}, f32[17,128]{1,0:T(8,128)S(1)}) custom-call(s32[1]{0:T(128)} %bitcast.tile_row_ref, s32[17]{0:T(128)S(1)} %copy-done.2, s32[4,32]{1,0:T(4,128)S(1)} %copy-done, s32[4,32]{1,0:T(4,128)S(1)} %copy-done.1), custom_call_target="tpu_custom_call" | custom-call | flops 1048576 | bytes 1048576 | tf_op jit(solution)/shard_map/pallas_call | solution.py:362
  9.9 22.9 %all-to-all-done.x_ref.refs_4_ = bf16[16,16,2048]{2,1,0:T(8,128)(2,1)S(1)} async-done(((bf16[16,16,2048]{2,1,0:T(8,128)(2,1)}), bf16[16,16,2048]{2,1,0:T(8,128)(2,1)S(1)}, u32[]{:S(2)}, u32[]{:S(2)}) %all-to-all-start) | async-done | bytes 1048608 | tf_op jit(solution)/shard_map/all_to_all | solution.py:356
  32.8 0.9 %shard_map.47.refs_0_ = f32[24,128]{1,0:T(8,128)S(1)} custom-call(bf16[16,16,2048]{2,1,0:T(8,128)(2,1)S(1)} %all-to-all-done.x_ref.refs_4_, bf16[256,128]{1,0:T(8,128)(2,1)S(1)} %get-tuple-element.12.pairing_ref), custom_call_target="tpu_custom_call" | custom-call | flops 4194304 | bytes 1048576 | tf_op jit(solution)/shard_map/pallas_call | solution.py:377
  33.6 2.0 %collective-permute-start.2 = (f32[24,128]{1,0:T(8,128)S(1)}, f32[24,128]{1,0:T(8,128)S(1)}, u32[]{:S(2)}, u32[]{:S(2)}) collective-permute-start(f32[24,128]{1,0:T(8,128)S(1)} %shard_map.47.refs_0_), channel_id=1, source_target_pairs={{0,6},{2,4},{4,2},{6,0},{8,14},{10,12},{12,10},{14,8},{16,22},{18,... | collective-permute-start | bytes 36872 | tf_op jit(solution)/shard_map/ppermute | solution.py:399
  35.6 0.1 collective-permute-start.1
  35.7 1.4 %collective-permute-start = (f32[24,128]{1,0:T(8,128)S(1)}, f32[24,128]{1,0:T(8,128)S(1)}, u32[]{:S(2)}, u32[]{:S(2)}) collective-permute-start(f32[24,128]{1,0:T(8,128)S(1)} %shard_map.47.refs_0_), channel_id=1, source_target_pairs={{0,2},{2,0},{4,6},{6,4},{8,10},{10,8},{12,14},{14,12},{16,18},{18,... | collective-permute-start | bytes 36872 | tf_op jit(solution)/shard_map/ppermute | solution.py:399
  37.2 1.1 %collective-permute-done.2.refs_3_ = f32[24,128]{1,0:T(8,128)S(1)} collective-permute-done((f32[24,128]{1,0:T(8,128)S(1)}, f32[24,128]{1,0:T(8,128)S(1)}, u32[]{:S(2)}, u32[]{:S(2)}) %collective-permute-start.2) | collective-permute-done | bytes 12320 | tf_op jit(solution)/shard_map/ppermute | solution.py:399
  38.3 1.1 %collective-permute-done.1.refs_2_ = f32[24,128]{1,0:T(8,128)S(1)} collective-permute-done((f32[24,128]{1,0:T(8,128)S(1)}, f32[24,128]{1,0:T(8,128)S(1)}, u32[]{:S(2)}, u32[]{:S(2)}) %collective-permute-start.1) | collective-permute-done | bytes 12320 | tf_op jit(solution)/shard_map/ppermute | solution.py:399
  39.3 0.1 collective-permute-done.refs_1_
  39.4 1.7 %shard_map.48 = bf16[16,16,2048]{2,1,0:T(8,128)(2,1)} custom-call(f32[16,128]{1,0:T(8,128)S(1)} %get-tuple-element.9.fraction_ref, f32[17,128]{1,0:T(8,128)S(1)} %get-tuple-element.10.curve_ref, bf16[128,2048]{1,0:T(8,128)(2,1)S(1)} %get-tuple-element.11.to_pixels_ref, f32[24,128]{1,0:T(8,128)S(1)} %shard_map.47.refs_0_, ...), custom_call_target="tpu_custom_call" | custom-call | flops 16777216 | bytes 2097152 | tf_op jit(solution)/shard_map/pallas_call | solution.py:403
Async XLA Ops:
  0.0 32.8 %all-to-all-start = ((bf16[16,16,2048]{2,1,0:T(8,128)(2,1)}), bf16[16,16,2048]{2,1,0:T(8,128)(2,1)S(1)}, u32[]{:S(2)}, u32[]{:S(2)}) async-start(bf16[16,16,2048]{2,1,0:T(8,128)(2,1)} %bitcast.2), calls=%async_computation | async-start | bytes 2097152 | tf_op jit(solution)/shard_map/all_to_all | solution.py:356
  8.3 0.7 %copy-start.1 = (s32[4,32]{1,0:T(4,128)S(1)}, s32[4,32]{1,0:T(4,128)}, u32[]{:S(2)}) copy-start(s32[4,32]{1,0:T(4,128)} %step_ref.1) | copy-start | bytes 1540
  8.3 0.7 %copy-start = (s32[4,32]{1,0:T(4,128)S(1)}, s32[4,32]{1,0:T(4,128)}, u32[]{:S(2)}) copy-start(s32[4,32]{1,0:T(4,128)} %offset_ref.1) | copy-start | bytes 1540
  8.4 0.7 %copy-start.2 = (s32[17]{0:T(128)S(1)}, s32[17]{0:T(128)}, u32[]{:S(2)}) copy-start(s32[17]{0:T(128)} %knots_ref.1) | copy-start | bytes 208
  33.6 4.6 %collective-permute-start.2 = (f32[24,128]{1,0:T(8,128)S(1)}, f32[24,128]{1,0:T(8,128)S(1)}, u32[]{:S(2)}, u32[]{:S(2)}) collective-permute-start(f32[24,128]{1,0:T(8,128)S(1)} %shard_map.47.refs_0_), channel_id=1, source_target_pairs={{0,6},{2,4},{4,2},{6,0},{8,14},{10,12},{12,10},{14,8},{16,22},{18,... | collective-permute-start | bytes 36872 | tf_op jit(solution)/shard_map/ppermute | solution.py:399
  35.6 3.7 %collective-permute-start.1 = (f32[24,128]{1,0:T(8,128)S(1)}, f32[24,128]{1,0:T(8,128)S(1)}, u32[]{:S(2)}, u32[]{:S(2)}) collective-permute-start(f32[24,128]{1,0:T(8,128)S(1)} %shard_map.47.refs_0_), channel_id=1, source_target_pairs={{0,4},{2,6},{4,0},{6,2},{8,12},{10,14},{12,8},{14,10},{16,20},{18,... | collective-permute-start | bytes 36872 | tf_op jit(solution)/shard_map/ppermute | solution.py:399
  35.7 3.7 %collective-permute-start = (f32[24,128]{1,0:T(8,128)S(1)}, f32[24,128]{1,0:T(8,128)S(1)}, u32[]{:S(2)}, u32[]{:S(2)}) collective-permute-start(f32[24,128]{1,0:T(8,128)S(1)} %shard_map.47.refs_0_), channel_id=1, source_target_pairs={{0,2},{2,0},{4,6},{6,4},{8,10},{10,8},{12,14},{14,12},{16,18},{18,... | collective-permute-start | bytes 36872 | tf_op jit(solution)/shard_map/ppermute | solution.py:399
